TPU v7x, 256 devices: a whole 4x4x8 slice. The times are simulated.
256 devices in a mesh: dp: 16 (over z, core), expert: 16 (over x, y).
Axes of the slice: x: 4, y: 4, z: 8, core: 2. Of those that a mesh axis runs over, the one named last changes fastest.
Arguments:
- tokens: bfloat16 [2048, 1440], P('expert'), may hold values from -6 to 6
- output_grad: bfloat16 [2048, 1440], P('expert'), may hold values from -6 to 6
- router_logits: float32 [2048, 4], P('expert'), may hold values from -4 to 4
- expert_ids: int32 [2048, 4], P('expert'), may hold values from 0 to 63, all different within a row; in each aligned block of 128 rows (0 to 127, 128 to 255, ...) at most 10 rows name the same one
- w_gate: bfloat16 [64, 1440, 2048], P('expert', None, 'dp'), may hold values from -0.21875 to 0.21875
- w_up: bfloat16 [64, 1440, 2048], P('expert', None, 'dp'), may hold values from -0.21875 to 0.21875
- w_down: bfloat16 [64, 2048, 1440], P('expert', 'dp'), may hold values from -0.1875 to 0.1875
Outputs:
- mixed: bfloat16 [2048, 1440], P('expert', 'dp')
- input_grad: bfloat16 [2048, 1440], P('expert', 'dp')
- router_grad: float32 [2048, 4], P('expert')
- grad_gate: bfloat16 [64, 1440, 2048], P('expert', None, 'dp')
- grad_up: bfloat16 [64, 1440, 2048], P('expert', None, 'dp')
- grad_down: bfloat16 [64, 2048, 1440], P('expert', 'dp')
Inputs may be any that keep to these rules, and one draw needn't show every extreme that they name: `expert_ids`: in each aligned block of 128 rows (the rows of one device), no expert is named more than 10 times, a bound that some block reaches.
All inputs are finite; a program needn't handle non-finite values.
Results may differ from a plain program's by a relative error of at most 0.0064.
Values may be sent and summed in bfloat16 or wider, within the bound.
A program may use at most 128 MiB of HBM per device.

v0:
```python
import jax
import jax.numpy as jnp
from jax import lax
from jax.sharding import PartitionSpec as P


def route_out(buffer):
    return lax.all_to_all(buffer, "expert", split_axis=0, concat_axis=0, tiled=True)


def route_back(buffer):
    return lax.all_to_all(buffer, "expert", split_axis=0, concat_axis=0, tiled=True)


def on_device(tokens, output_grad, router_logits, expert_ids, w_gate, w_up, w_down):
    group_size = lax.axis_size("expert")
    local_experts = w_gate.shape[0]
    tok_rows = tokens.shape[0]
    feat_full = tokens.shape[1]
    feat_local = feat_full // lax.axis_size("dp")
    dp_index = lax.axis_index("dp")
    top_picks = expert_ids.shape[1]
    all_experts = local_experts * group_size
    num_picks = tok_rows * top_picks
    capacity = 5 * tok_rows * top_picks // (4 * all_experts)
    lifted = jnp.exp(router_logits)
    weights = lifted / jnp.sum(lifted, -1, keepdims=True)
    flat_ids = expert_ids.reshape(-1)
    one_hot = (flat_ids[:, None] == jnp.arange(all_experts, dtype=jnp.int32)[None, :]).astype(
        jnp.int32
    )
    before = jnp.cumsum(one_hot, 0) - one_hot
    pick_rank = jnp.sum(before * one_hot, 1)
    slot_of = flat_ids * capacity + pick_rank
    slot_table = jnp.full((all_experts * capacity,), num_picks, jnp.int32)
    slot_table = slot_table.at[slot_of].set(jnp.arange(num_picks, dtype=jnp.int32))
    zero_row = jnp.zeros((1, feat_full), jnp.bfloat16)
    padded_tokens = jnp.concatenate([tokens, zero_row], 0)
    buffer_shape = (group_size, local_experts, capacity, feat_full)
    send_rows = padded_tokens[slot_table // top_picks].reshape(buffer_shape)
    scaled = weights.reshape(-1, 1) * jnp.repeat(output_grad, top_picks, axis=0).astype(jnp.float32)
    padded_grads = jnp.concatenate([scaled.astype(jnp.bfloat16), zero_row], 0)
    send_grads = padded_grads[slot_table].reshape(buffer_shape)
    rows_recv = route_out(send_rows)
    grads_recv = route_out(send_grads)
    pre_gate = jnp.einsum("secd,edf->secf", rows_recv, w_gate, preferred_element_type=jnp.float32)
    pre_up = jnp.einsum("secd,edf->secf", rows_recv, w_up, preferred_element_type=jnp.float32)
    sigmoid_gate = jax.nn.sigmoid(1.702 * pre_gate)
    activated = pre_gate * sigmoid_gate
    hidden = (activated * (pre_up + 1.0)).astype(jnp.bfloat16)
    out_terms = jnp.einsum("secf,efd->secd", hidden, w_down, preferred_element_type=jnp.float32)
    expert_sum = None
    expert_sum = lax.psum_scatter(out_terms, "dp", scatter_dimension=3, tiled=True)
    hidden_grad = jnp.einsum(
        "secd,efd->secf", grads_recv, w_down, preferred_element_type=jnp.float32
    )
    slope = sigmoid_gate + 1.702 * pre_gate * sigmoid_gate * (1.0 - sigmoid_gate)
    gate_grad = (hidden_grad * (pre_up + 1.0) * slope).astype(jnp.bfloat16)
    up_grad = (hidden_grad * activated).astype(jnp.bfloat16)
    grad_down = jnp.einsum(
        "secf,secd->efd", hidden, grads_recv, preferred_element_type=jnp.float32
    ).astype(jnp.bfloat16)
    both_grads = jnp.concatenate([gate_grad, up_grad], -1)
    joint_grad = jnp.einsum(
        "secd,secf->edf", rows_recv, both_grads, preferred_element_type=jnp.float32
    )
    hidden_local = w_gate.shape[2]
    grad_gate = joint_grad[:, :, :hidden_local].astype(jnp.bfloat16)
    grad_up = joint_grad[:, :, hidden_local:].astype(jnp.bfloat16)
    input_terms = jnp.einsum(
        "secf,edf->secd", gate_grad, w_gate, preferred_element_type=jnp.float32
    ) + jnp.einsum("secf,edf->secd", up_grad, w_up, preferred_element_type=jnp.float32)
    input_sum = lax.psum_scatter(input_terms, "dp", scatter_dimension=3, tiled=True)
    expert_out = expert_sum.astype(jnp.bfloat16)
    out_back = route_back(expert_out).reshape(all_experts * capacity, feat_local)
    out_pick = out_back[slot_of].reshape(tok_rows, top_picks, feat_local).astype(jnp.float32)
    mixed = jnp.sum(weights[:, :, None] * out_pick, 1).astype(jnp.bfloat16)
    own_grad = lax.dynamic_slice_in_dim(output_grad, dp_index * feat_local, feat_local, 1)
    partial_dots = jnp.sum(own_grad.astype(jnp.float32)[:, None, :] * out_pick, -1)
    pick_dot = lax.psum(partial_dots, "dp")
    router_grad = weights * (pick_dot - jnp.sum(weights * pick_dot, -1, keepdims=True))
    slot_grad = input_sum.astype(jnp.bfloat16)
    grad_back = route_back(slot_grad).reshape(all_experts * capacity, feat_local)
    grad_pick = grad_back[slot_of].reshape(tok_rows, top_picks, feat_local).astype(jnp.float32)
    input_grad = jnp.sum(grad_pick, 1).astype(jnp.bfloat16)
    return (mixed, input_grad, router_grad, grad_gate, grad_up, grad_down)


def solution(mesh):
    in_specs = (
        P("expert", None),
        P("expert", None),
        P("expert", None),
        P("expert", None),
        P("expert", None, "dp"),
        P("expert", None, "dp"),
        P("expert", "dp", None),
    )
    out_specs = (
        P("expert", "dp"),
        P("expert", "dp"),
        P("expert", None),
        P("expert", None, "dp"),
        P("expert", None, "dp"),
        P("expert", "dp", None),
    )
    return jax.shard_map(
        on_device, mesh=mesh, in_specs=in_specs, out_specs=out_specs, check_vma=False
    )
```

profile of v0, /device:TPU:1, one launch (start us, length us, event | category | flops | bytes accessed | tf_op | source)
XLA Modules:
  0.0 261.1 jit_solution(4399466944299262114)
XLA Ops:
  0.6 0.8 broadcast_multiply_fusion
  1.4 0.8 copy.78
  2.4 1.2 copy.76
  3.9 1.2 reduce-window.6
  5.5 2.4 scatter_custom_fusion
  8.0 3.7 %gather_fusion = bf16[640,1440]{1,0:T(8,128)(2,1)} fusion(bf16[129,1440]{1,0:T(8,128)(2,1)S(1)} %concatenate.9, s32[1024]{0:T(1024)S(1)} %get-tuple-element.36), kind=kCustom, calls=%fused_computation | custom fusion | bytes 3688960 | tf_op jit(solution)/shard_map/gather | solution.py:40
  11.7 4.3 %reshape.95 = bf16[16,4,10,1440]{3,2,1,0:T(8,128)(2,1)} reshape(bf16[640,1440]{1,0:T(8,128)(2,1)} %gather_fusion) | data formatting | bytes 3686400 | tf_op jit(solution)/shard_map/reshape | solution.py:40
  16.0 4.9 %copy.81 = bf16[16,4,10,1440]{3,1,2,0:T(4,128)(2,1)} copy(bf16[16,4,10,1440]{3,2,1,0:T(8,128)(2,1)} %reshape.95) | data formatting | bytes 3686400 | tf_op jit(solution)/shard_map/reshape | solution.py:40
  20.9 7.8 %all-to-all-start = ((bf16[16,4,10,1440]{3,1,2,0:T(4,128)(2,1)}), bf16[16,4,10,1440]{3,1,2,0:T(4,128)(2,1)}, u32[]{:S(2)}, u32[]{:S(2)}) async-start(bf16[16,4,10,1440]{3,1,2,0:T(4,128)(2,1)} %copy.81), calls=%async_computation | async-start | bytes 3932160 | tf_op jit(solution)/shard_map/all_to_all | solution.py:8
  28.8 2.2 broadcast_in_dim.10
  31.1 4.9 %convert_element_type.63 = f32[512,1440]{1,0:T(8,128)} reshape(f32[128,4,1440]{2,1,0:T(4,128)} %broadcast_in_dim.10) | data formatting | bytes 5898240 | tf_op jit(solution)/shard_map/convert_element_type | solution.py:41
  36.4 0.5 copy-done.5
  36.9 2.1 multiply_convert_fusion
  39.2 3.7 %gather_fusion.2 = bf16[640,1440]{1,0:T(8,128)(2,1)} fusion(bf16[513,1440]{1,0:T(8,128)(2,1)S(1)} %concatenate.10, s32[1024]{0:T(1024)S(1)} %get-tuple-element.35), kind=kCustom, calls=%fused_computation.2 | custom fusion | bytes 3688960 | tf_op jit(solution)/shard_map/gather | solution.py:43
  42.9 4.3 %reshape.97 = bf16[16,4,10,1440]{3,2,1,0:T(8,128)(2,1)} reshape(bf16[640,1440]{1,0:T(8,128)(2,1)} %gather_fusion.2) | data formatting | bytes 3686400 | tf_op jit(solution)/shard_map/reshape | solution.py:43
  47.1 4.8 %copy.89 = bf16[16,4,10,1440]{3,1,2,0:T(4,128)(2,1)} copy(bf16[16,4,10,1440]{3,2,1,0:T(8,128)(2,1)} %reshape.97) | data formatting | bytes 3686400 | tf_op jit(solution)/shard_map/reshape | solution.py:43
  52.0 2.6 all-to-all-done
  54.6 4.6 %all-to-all-start.2 = ((bf16[16,4,10,1440]{3,1,2,0:T(4,128)(2,1)}), bf16[16,4,10,1440]{3,1,2,0:T(4,128)(2,1)S(1)}, u32[]{:S(2)}, u32[]{:S(2)}) async-start(bf16[16,4,10,1440]{3,1,2,0:T(4,128)(2,1)} %copy.89), calls=%async_computation.2 | async-start | bytes 3932160 | tf_op jit(solution)/shard_map/all_to_all | solution.py:8
  59.2 0.8 dynamic-slice_convert_fusion.2
  59.9 0.7 copy.94
  60.6 1.3 dynamic-slice
  62.5 0.7 pad_clamp_fusion.1
  63.2 4.1 %fusion.26 = f32[16,4,10,128]{3,0,2,1:T(8,128)} fusion(bf16[4,1440,128]{2,1,0:T(8,128)(2,1)} %param.11, bf16[16,4,10,1440]{3,1,2,0:T(4,128)(2,1)} %all-to-all-done), kind=kOutput, calls=%fused_computation.28 | convolution fusion | flops 235929600 | bytes 3645440 | tf_op jit(solution)/shard_map/secd,edf->secf/dot_general | solution.py:46
  67.3 3.7 %fusion.21 = f32[16,4,10,128]{3,0,2,1:T(8,128)} fusion(bf16[4,1440,128]{2,1,0:T(8,128)(2,1)S(1)} %copy-done.1, bf16[16,4,10,1440]{3,1,2,0:T(4,128)(2,1)} %all-to-all-done), kind=kOutput, calls=%fused_computation.27 | convolution fusion | flops 236011520 | bytes 3645440 | tf_op jit(solution)/shard_map/secd,edf->secf/dot_general | solution.py:47
  71.0 12.1 %all-to-all-done.2 = bf16[16,4,10,1440]{3,1,2,0:T(4,128)(2,1)S(1)} async-done(((bf16[16,4,10,1440]{3,1,2,0:T(4,128)(2,1)}), bf16[16,4,10,1440]{3,1,2,0:T(4,128)(2,1)S(1)}, u32[]{:S(2)}, u32[]{:S(2)}) %all-to-all-start.2) | async-done | bytes 1843232 | tf_op jit(solution)/shard_map/all_to_all | solution.py:8
  83.1 3.2 %multiply_convert_fusion.1 = (bf16[16,4,10,128]{3,0,2,1:T(8,128)(2,1)}, bf16[16,4,10,128]{3,0,2,1:T(8,128)(2,1)}, bf16[16,4,10,128]{3,0,2,1:T(8,128)(2,1)S(1)}) fusion(f32[16,4,10,128]{3,0,2,1:T(8,128)} %fusion.26, f32[16,4,10,128]{3,0,2,1:T(8,128)} %fusion.21, bf16[4,128,1440]{1,2,0:T(8,128)(2,1)S(1)} %copy-done, ...), kind=kOutput, calls=%fused_computation.37 | convolution fusion | flops 237240320 | bytes 4464640 | tf_op jit(solution)/shard_map/secd,efd->secf/dot_general | solution.py:54
  86.3 0.7 copy-done.3
  86.9 2.6 convolution_bitcast_fusion
  89.5 68.6 %all-reduce.7 = bf16[16,4,10,1440]{3,0,2,1:T(8,128)(2,1)} all-reduce(f32[16,4,10,1440]{3,0,2,1:T(8,128)} %convolution_bitcast_fusion), channel_id=2, replica_groups=mesh['dp'=16,'expert'=16] {'dp'}, use_global_device_ids=true, to_apply=%region_5.6.clone | all-reduce | flops 921600 | bytes 5529600
  158.1 1.1 dynamic-slice_convert_fusion.1
  159.2 0.7 copy.86
  159.9 4.2 %all-to-all-start.1 = ((bf16[16,4,10,90]{3,1,2,0:T(4,128)(2,1)}), bf16[16,4,10,90]{3,1,2,0:T(4,128)(2,1)}, u32[]{:S(2)}, u32[]{:S(2)}) async-start(bf16[16,4,10,90]{3,1,2,0:T(4,128)(2,1)} %copy.86), calls=%async_computation.1 | async-start | bytes 327680 | tf_op jit(solution)/shard_map/all_to_all | solution.py:12
  164.1 2.2 fusion.11
  166.4 2.6 add_bitcast_fusion
  169.0 3.0 %bitcast_convert_fusion = bf16[4,1440,256]{2,1,0:T(8,128)(2,1)S(1)} fusion(bf16[16,4,10,1440]{3,1,2,0:T(4,128)(2,1)} %all-to-all-done, bf16[16,4,10,128]{3,0,2,1:T(8,128)(2,1)S(1)} %copy-done.10, bf16[16,4,10,128]{3,0,2,1:T(8,128)(2,1)S(1)} %copy-done.9), kind=kOutput, calls=%fused_computation.5 | convolution fusion | flops 473989120 | bytes 5120000 | tf_op jit(solution)/shard_map/secd,secf->edf/dot_general | solution.py:64
  172.0 2.1 fusion.51
  174.1 2.6 %fusion = bf16[4,128,1440]{1,2,0:T(8,128)(2,1)} fusion(bf16[16,4,10,128]{3,0,2,1:T(8,128)(2,1)S(1)} %copy-done.4, bf16[16,4,10,1440]{3,1,2,0:T(4,128)(2,1)S(1)} %all-to-all-done.2), kind=kOutput, calls=%fused_computation.10 | convolution fusion | flops 236666880 | bytes 3481600 | tf_op jit(solution)/shard_map/secf,secd->efd/dot_general | solution.py:60
  176.7 1.0 copy.87
  177.9 1.3 gather_fusion.1
  179.7 63.5 %all-reduce.8 = (bf16[16,4,10,1440]{3,0,2,1:T(8,128)(2,1)}, f32[128,4]{1,0:T(8,128)S(1)}) all-reduce(f32[16,4,10,1440]{3,0,2,1:T(8,128)} %add_bitcast_fusion, f32[128,4]{1,0:T(8,128)S(1)} %get-tuple-element.24), channel_id=3, replica_groups=mesh['dp'=16,'expert'=16] {'dp'}, use_global_device_ids=true, to_apply=%region_7.8.clone | all-reduce | flops 922112 | bytes 5533696
  243.2 1.1 dynamic-slice_convert_fusion
  244.3 0.7 copy.92
  245.0 6.8 %all-to-all-start.3 = ((bf16[16,4,10,90]{3,1,2,0:T(4,128)(2,1)}), bf16[16,4,10,90]{3,1,2,0:T(4,128)(2,1)S(1)}, u32[]{:S(2)}, u32[]{:S(2)}) async-start(bf16[16,4,10,90]{3,1,2,0:T(4,128)(2,1)} %copy.92), calls=%async_computation.3 | async-start | bytes 327680 | tf_op jit(solution)/shard_map/all_to_all | solution.py:12
  252.2 0.7 copy.99
  252.9 0.7 copy.101
  253.5 5.1 %all-to-all-done.3 = bf16[16,4,10,90]{3,1,2,0:T(4,128)(2,1)S(1)} async-done(((bf16[16,4,10,90]{3,1,2,0:T(4,128)(2,1)}), bf16[16,4,10,90]{3,1,2,0:T(4,128)(2,1)S(1)}, u32[]{:S(2)}, u32[]{:S(2)}) %all-to-all-start.3) | async-done | bytes 115232 | tf_op jit(solution)/shard_map/all_to_all | solution.py:12
  258.8 1.3 gather_fusion.3
  260.4 0.7 copy.100
  (56 shorter events, 2.9 us)
Async XLA Ops:
  0.6 82.5 %copy-start = (bf16[4,128,1440]{1,2,0:T(8,128)(2,1)S(1)}, bf16[4,128,1440]{1,2,0:T(8,128)(2,1)}, u32[]{:S(2)}) copy-start(bf16[4,128,1440]{1,2,0:T(8,128)(2,1)} %param.13) | copy-start | bytes 4423684
  5.5 2.5 copy-start.13
  20.9 7.8 %copy-start.7 = (bf16[128,1440]{0,1:T(8,128)(2,1)S(1)}, bf16[128,1440]{0,1:T(8,128)(2,1)}, u32[]{:S(2)}) copy-start(bf16[128,1440]{0,1:T(8,128)(2,1)} %param.8) | copy-start | bytes 1105924
  20.9 33.7 %all-to-all-start = ((bf16[16,4,10,1440]{3,1,2,0:T(4,128)(2,1)}), bf16[16,4,10,1440]{3,1,2,0:T(4,128)(2,1)}, u32[]{:S(2)}, u32[]{:S(2)}) async-start(bf16[16,4,10,1440]{3,1,2,0:T(4,128)(2,1)} %copy.81), calls=%async_computation | async-start | bytes 3932160 | tf_op jit(solution)/shard_map/all_to_all | solution.py:8
  31.1 4.9 %copy-start.14 = (f32[128,4]{0,1:T(4,128)S(1)}, f32[128,4]{0,1:T(4,128)}, u32[]{:S(2)}) copy-start(f32[128,4]{0,1:T(4,128)} %param.9) | copy-start | bytes 6148
  36.2 2.9 %copy-start.11 = (f32[128]{0:T(128)}, f32[128]{0:T(128)S(1)}, u32[]{:S(2)}) copy-start(f32[128]{0:T(128)S(1)} %exponential_reduce_fusion) | copy-start | bytes 1540
  36.3 0.6 copy-start.5
  54.6 28.5 %all-to-all-start.2 = ((bf16[16,4,10,1440]{3,1,2,0:T(4,128)(2,1)}), bf16[16,4,10,1440]{3,1,2,0:T(4,128)(2,1)S(1)}, u32[]{:S(2)}, u32[]{:S(2)}) async-start(bf16[16,4,10,1440]{3,1,2,0:T(4,128)(2,1)} %copy.89), calls=%async_computation.2 | async-start | bytes 3932160 | tf_op jit(solution)/shard_map/all_to_all | solution.py:8
  63.2 4.1 %copy-start.1 = (bf16[4,1440,128]{2,1,0:T(8,128)(2,1)S(1)}, bf16[4,1440,128]{2,1,0:T(8,128)(2,1)}, u32[]{:S(2)}) copy-start(bf16[4,1440,128]{2,1,0:T(8,128)(2,1)} %param.12) | copy-start | bytes 4423684
  86.3 0.7 copy-start.3
  159.9 16.8 %all-to-all-start.1 = ((bf16[16,4,10,90]{3,1,2,0:T(4,128)(2,1)}), bf16[16,4,10,90]{3,1,2,0:T(4,128)(2,1)}, u32[]{:S(2)}, u32[]{:S(2)}) async-start(bf16[16,4,10,90]{3,1,2,0:T(4,128)(2,1)} %copy.86), calls=%async_computation.1 | async-start | bytes 327680 | tf_op jit(solution)/shard_map/all_to_all | solution.py:12
  164.1 2.3 copy-start.2
  164.1 2.3 copy-start.10
  166.4 2.6 copy-start.9
  172.0 2.1 copy-start.4
  176.7 2.5 copy-start.6
  176.7 2.5 copy-start.8
  179.7 72.2 %copy-start.12 = (f32[128]{0:T(128)S(1)}, f32[128]{0:T(128)}, u32[]{:S(2)}) copy-start(f32[128]{0:T(128)} %copy-done.11) | copy-start | bytes 1540
  245.0 13.6 %all-to-all-start.3 = ((bf16[16,4,10,90]{3,1,2,0:T(4,128)(2,1)}), bf16[16,4,10,90]{3,1,2,0:T(4,128)(2,1)S(1)}, u32[]{:S(2)}, u32[]{:S(2)}) async-start(bf16[16,4,10,90]{3,1,2,0:T(4,128)(2,1)} %copy.92), calls=%async_computation.3 | async-start | bytes 327680 | tf_op jit(solution)/shard_map/all_to_all | solution.py:12
where the time goes:
time: 264 us; the launch traced here: 261 us
  blocking collectives  132 us (50%)
  local copies, waits for them, and re-layouts  53.3 us (20%)
  matrix products  24 us (9%)
  starting transfers between devices  23.3 us (9%)
  waiting for transfers between devices  19.8 us (8%)
  other arithmetic  6.91 us (3%)
    unnamed x2, blocking collectives  132 us
    all_to_all x2, waiting for transfers between devices, route_out(): lax.all_to_all(buffer, 'expert', split_axis=0, concat_axis=0, tiled=True)  14.6 us
    all_to_all x2, starting transfers between devices, route_out(): lax.all_to_all(buffer, 'expert', split_axis=0, concat_axis=0, tiled=True)  12.3 us
    all_to_all x2, starting transfers between devices, route_back(): lax.all_to_all(buffer, 'expert', split_axis=0, concat_axis=0, tiled=True)  11 us
    reshape x2, local copies, waits for them, and re-layouts, on_device(): send_rows = padded_tokens[slot_table // top_picks].reshape(buffer_shape)  9.15 us
    reshape x2, local copies, waits for them, and re-layouts, on_device(): send_grads = padded_grads[slot_table].reshape(buffer_shape)  9.11 us
    unnamed x37, local copies, waits for them, and re-layouts  6.65 us
  transfers between devices with their start and end apart: 4, of which 3 were waited for; matrix products, arithmetic and copies ran while one was open for 18% of the time, Pallas kernels for 0%

commit v1 on v0

v1 whole, which is shorter than its diff:
```python
import functools

import jax
import jax.numpy as jnp
from jax import lax
from jax.experimental import pallas as pl
from jax.experimental.pallas import tpu as pltpu
from jax.sharding import PartitionSpec as P

MESH = pl.DeviceIdType.MESH
F32 = jnp.float32
BF16 = jnp.bfloat16

D = 1440
HALF = 720
WIDE = 768
PADDED = 1536
HID = 128
TOK = 128
RANKS = 10
SRC = 16
ROWS = SRC * RANKS
PAIR = 2 * ROWS
SLAB = 16
MSG = 1024
GROUP = 256
BLK = 90
BROWS = 96


def dg(a, b, ca, cb):
    return lax.dot_general(a, b, (((ca,), (cb,)), ((), ())), preferred_element_type=F32)


def iota(shape, dim):
    return lax.broadcasted_iota(jnp.int32, shape, dim)


def ones_where(mask):
    return jnp.where(mask, 1.0, 0.0).astype(BF16)


def kernel(
    tok_hbm, og_hbm, logits_ref, ids_ref, wg_hbm, wu_hbm, wd_hbm,
    mixed_ref, igrad_ref, rgrad_ref, gg_hbm, gu_hbm, gd_hbm,
    tok, og, wg, wu, wd,
    send_slab, cat, rows, sel_main, sel_fold, comb_hi, comb_lo, comb_one,
    grp, ungrp, blksel,
    sig, pre, act, upp, hid, ggu,
    part, crecv, zsend, zrecv, slab, back, blocks, frecv, dots,
    grads,
    in_sem, xy_s, xy_r, zf_s, zf_r, cf_s, cf_r, rc_s, rc_r, rz_s, rz_r,
    bk_s, bk_r, fb_s, fb_r, dt_s, dt_r, out_sem,
):
    d = lax.axis_index("dp")
    me = lax.axis_index("expert")
    z, c = lax.div(d, 2), lax.rem(d, 2)
    x, y = lax.div(me, 4), lax.rem(me, 4)
    par = lax.rem(z, 2)
    sib = (z * 2 + 1 - c, me)
    up = (lax.rem(z + 1, 8) * 2 + c, me)
    down = (lax.rem(z + 7, 8) * 2 + c, me)

    def peer(i):
        return lax.rem(x + i // 4, 4) * 4 + lax.rem(y + i % 4, 4)

    def origin(i):
        return lax.rem(x + 4 - i // 4, 4) * 4 + lax.rem(y + 4 - i % 4, 4)

    def slab_rows(s):
        return pl.ds(pl.multiple_of(s * SLAB, SLAB), SLAB)

    barrier = pltpu.get_barrier_semaphore()

    def greet(i, carry):
        pl.semaphore_signal(barrier, inc=1, device_id=(d, peer(i)), device_id_type=MESH)
        pl.semaphore_signal(
            barrier, inc=1, device_id=(lax.rem(d + i, 16), me), device_id_type=MESH
        )
        return carry

    lax.fori_loop(1, 16, greet, 0)

    loads = [
        pltpu.make_async_copy(tok_hbm, tok.at[pl.ds(0, D)], in_sem.at[0]),
        pltpu.make_async_copy(og_hbm, og.at[pl.ds(0, D)], in_sem.at[1]),
    ]
    for n, (src, dst) in enumerate(((wg_hbm, wg), (wu_hbm, wu), (wd_hbm, wd))):
        for e in range(4):
            loads.append(
                pltpu.make_async_copy(src.at[e], dst.at[e, pl.ds(0, D)], in_sem.at[2 + 4 * n + e])
            )
    for load in loads:
        load.start()
    tok[pl.ds(D, PADDED - D), :] = jnp.zeros((PADDED - D, TOK), BF16)
    og[pl.ds(D, PADDED - D), :] = jnp.zeros((PADDED - D, TOK), BF16)
    for w in (wg, wu, wd):
        for e in range(4):
            w[e, pl.ds(D, WIDE - HALF), :] = jnp.zeros((WIDE - HALF, HID), BF16)

    lifted = jnp.exp(logits_ref[...])
    weights = lifted / jnp.sum(lifted, 0, keepdims=True)
    ids = ids_ref[...]
    row = iota((256, TOK), 0)
    spot = row & 15
    earlier = ones_where(iota((TOK, TOK), 0) < iota((TOK, TOK), 1))

    def select(expert, rank):
        named = jnp.zeros((256, TOK), F32)
        weigh = jnp.zeros((256, TOK), F32)
        for p in range(4):
            same = ids[p : p + 1, :] == expert
            named = jnp.where(same, 1.0, named)
            weigh = jnp.where(same, weights[p : p + 1, :], weigh)
        before = dg(named.astype(BF16), earlier, 1, 0)
        chosen = (before == rank.astype(F32)) & (named > 0.5)
        return chosen, jnp.where(chosen, weigh, 0.0)

    second = jnp.where(spot >= RANKS, 1, 0)
    base = 4 * (row >> 4) + 2 * par
    main_expert = base + second
    fold_expert = base + 1
    main, main_w = select(main_expert, spot - RANKS * second)
    fold, fold_w = select(fold_expert, 6 + (spot & 3))
    sel_main[...] = ones_where(main)
    comb_hi[0] = main_w.astype(BF16)
    comb_lo[0] = (main_w - main_w.astype(BF16).astype(F32)).astype(BF16)
    comb_one[0] = ones_where(main)
    for k in range(3):
        here = (spot >> 2) == k
        sel_fold[:, k * TOK : (k + 1) * TOK] = ones_where(fold & here)
        w_here = jnp.where(here, fold_w, 0.0)
        comb_hi[1 + k] = w_here.astype(BF16)
        comb_lo[1 + k] = (w_here - w_here.astype(BF16).astype(F32)).astype(BF16)
        comb_one[1 + k] = ones_where(fold & here)
    main_scale = jnp.sum(main_w, 1, keepdims=True)
    fold_scale = jnp.sum(jnp.where((spot >> 2) < 3, fold_w, 0.0), 1, keepdims=True)

    start = pl.multiple_of(c * WIDE, WIDE)
    for a, source in enumerate((tok, og)):
        loads[a].wait()
        feats = source[pl.ds(start, WIDE), :]
        whole = dg(sel_main[...], feats, 1, 1)
        folded = jnp.zeros((256, GROUP), F32)
        for k in range(3):
            folded += dg(
                sel_fold[:, k * TOK : (k + 1) * TOK], feats[k * GROUP : (k + 1) * GROUP, :], 1, 1
            )
        if a == 1:
            whole = main_scale * whole
            folded = fold_scale * folded
        send_slab[a, :, 0:WIDE] = whole.astype(BF16)
        send_slab[a, :, WIDE:MSG] = folded.astype(BF16)

    pl.semaphore_wait(barrier, 30)

    def dispatch(a, i):
        return pltpu.make_async_remote_copy(
            src_ref=send_slab.at[a, slab_rows(peer(i))],
            dst_ref=cat.at[a, 0, c, slab_rows(me)],
            send_sem=xy_s.at[a, i], recv_sem=xy_r.at[a, i],
            device_id=(d, peer(i)), device_id_type=MESH,
        )

    def arrive(a, i):
        return pltpu.make_async_remote_copy(
            src_ref=send_slab.at[a, slab_rows(peer(i))],
            dst_ref=cat.at[a, 0, c, slab_rows(origin(i))],
            send_sem=xy_s.at[a, i], recv_sem=xy_r.at[a, i],
            device_id=(d, peer(i)), device_id_type=MESH,
        )

    def along_z(a, s):
        side = 1 - 2 * (s // 8)
        return pltpu.make_async_remote_copy(
            src_ref=cat.at[a, 0, c, slab_rows(s)],
            dst_ref=cat.at[a, 1, c, slab_rows(s)],
            send_sem=zf_s.at[a, s], recv_sem=zf_r.at[a, s],
            device_id=(lax.rem(z + side + 8, 8) * 2 + c, me), device_id_type=MESH,
        )

    def to_sibling(a, o, s):
        return pltpu.make_async_remote_copy(
            src_ref=cat.at[a, o, c, slab_rows(s)],
            dst_ref=cat.at[a, o, c, slab_rows(s)],
            send_sem=cf_s.at[a, o, s], recv_sem=cf_r.at[a, o, s],
            device_id=sib, device_id_type=MESH,
        )

    def from_sibling(a, o, s):
        return pltpu.make_async_remote_copy(
            src_ref=cat.at[a, o, c, slab_rows(s)],
            dst_ref=cat.at[a, o, 1 - c, slab_rows(s)],
            send_sem=cf_s.at[a, o, s], recv_sem=cf_r.at[a, o, s],
            device_id=sib, device_id_type=MESH,
        )

    def loop(lo, hi, body):
        def step(i, carry):
            body(i)
            return carry

        lax.fori_loop(lo, hi, step, 0)

    for a in range(2):
        cat[a, 0, c, slab_rows(me), :] = send_slab[a, slab_rows(me), :]
        loop(1, 16, lambda i, a=a: dispatch(a, i).start())

    n = iota((PAIR, 256), 0)
    i = iota((PAIR, 256), 1)
    later = jnp.where(n >= ROWS, 1, 0)
    m = n - ROWS * later
    s = (m * 6554) >> 16
    q = m - RANKS * s + RANKS * later
    grp[0] = ones_where((i == s * SLAB + q) & (q < 16))
    for k in range(3):
        grp[1 + k] = ones_where((i == s * SLAB + 4 * k + q - 16) & (q >= 16))
    n = iota((256, PAIR), 1)
    i = iota((256, PAIR), 0)
    later = jnp.where(n >= ROWS, 1, 0)
    m = n - ROWS * later
    s = (m * 6554) >> 16
    q = m - RANKS * s + RANKS * later
    ungrp[0] = ones_where((i == s * SLAB + q) & (q < 16))
    for k in range(3):
        ungrp[1 + k] = ones_where((i == s * SLAB + 4 * k + q - 16) & (q >= 16))
    line = iota((8 * BROWS, WIDE), 0)
    block = (line * 683) >> 16
    inner = line - BROWS * block
    blksel[...] = ones_where((iota((8 * BROWS, WIDE), 1) == BLK * block + inner) & (inner < BLK))

    def first_hop(a, lo, hi):
        def body(i):
            @pl.when(i > 0)
            def _():
                arrive(a, i).wait_recv()

            along_z(a, origin(i)).start()
            to_sibling(a, 0, origin(i)).start()

        loop(lo, hi, body)

    def second_hop(a):
        def body(s):
            along_z(a, s).wait_recv()
            to_sibling(a, 1, s).start()

        loop(0, 16, body)

    def regroup(a, o):
        loop(0, 16, lambda s: from_sibling(a, o, s).wait_recv())
        for h in range(2):
            folded = cat[a, o, h, :, WIDE:MSG]
            for k in range(3):
                value = dg(grp[0], cat[a, o, h, :, k * GROUP : (k + 1) * GROUP], 1, 0)
                value += dg(grp[1 + k], folded, 1, 0)
                rows[a, o, :, h * WIDE + k * GROUP : h * WIDE + (k + 1) * GROUP] = value.astype(BF16)

    def expert_of(o, le):
        return 2 * (par + o - 2 * par * o) + le

    def of_expert(le):
        return pl.ds(pl.multiple_of(le * ROWS, ROWS), ROWS)

    mine = pl.multiple_of(c * HALF, HALF)
    other = pl.multiple_of((1 - c) * HALF, HALF)

    def to_core(a, o):
        return pltpu.make_async_remote_copy(
            src_ref=part.at[a, 1, o], dst_ref=crecv.at[a, o],
            send_sem=rc_s.at[a, o], recv_sem=rc_r.at[a, o],
            device_id=sib, device_id_type=MESH,
        )

    def forward(o):
        regroup(0, o)

        def body(le):
            e = expert_of(o, le)
            r = of_expert(le)
            xe = rows[0, o, r, 0:D]
            pg = dg(xe, wg[e, pl.ds(0, D), :], 1, 0)
            pu = dg(xe, wu[e, pl.ds(0, D), :], 1, 0) + 1.0
            sg = jax.nn.sigmoid(1.702 * pg)
            ac = pg * sg
            sig[o, r, :] = sg
            pre[o, r, :] = pg
            act[o, r, :] = ac
            upp[o, r, :] = pu
            hd = (ac * pu).astype(BF16)
            hid[o, r, :] = hd
            part[0, 0, o, r, :] = dg(hd, wd[e, pl.ds(mine, WIDE), :], 1, 1).astype(BF16)
            part[0, 1, o, r, :] = dg(hd, wd[e, pl.ds(other, WIDE), :], 1, 1).astype(BF16)

        loop(0, 2, body)
        to_core(0, o).start()

    def backward(o):
        regroup(1, o)

        def body(le):
            e = expert_of(o, le)
            r = of_expert(le)
            ge = rows[1, o, r, 0:D]
            hg = dg(ge, wd[e, pl.ds(0, D), :], 1, 0)
            sg, pg, ac, pu = sig[o, r, :], pre[o, r, :], act[o, r, :], upp[o, r, :]
            slope = sg + 1.702 * pg * sg * (1.0 - sg)
            gate = (hg * pu * slope).astype(BF16)
            upg = (hg * ac).astype(BF16)
            ggu[o, r, 0:HID] = gate
            ggu[o, r, HID : 2 * HID] = upg
            dot = jnp.sum(hid[o, r, :].astype(F32) * hg, 1, keepdims=True)
            own = dg(gate, wg[e, pl.ds(mine, WIDE), :], 1, 1)
            own += dg(upg, wu[e, pl.ds(mine, WIDE), :], 1, 1)
            part[1, 0, o, r, :] = jnp.where(iota((ROWS, WIDE), 1) == HALF, dot, own).astype(BF16)
            far = dg(gate, wg[e, pl.ds(other, WIDE), :], 1, 1)
            far += dg(upg, wu[e, pl.ds(other, WIDE), :], 1, 1)
            part[1, 1, o, r, :] = jnp.where(iota((ROWS, WIDE), 1) == HALF, 0.0, far).astype(BF16)

        loop(0, 2, body)
        to_core(1, o).start()

    def across(a, le):
        return pltpu.make_async_remote_copy(
            src_ref=zsend.at[a, le], dst_ref=zrecv.at[a, le],
            send_sem=rz_s.at[a, le], recv_sem=rz_r.at[a, le],
            device_id=up if le == 0 else down, device_id_type=MESH,
        )

    def reduce_far(a):
        to_core(a, 1).wait_recv()
        for le in range(2):
            r = pl.ds(le * ROWS, ROWS)
            total = part[a, 0, 1, r, :].astype(F32) + crecv[a, 1, r, :].astype(F32)
            zsend[a, le] = total.astype(BF16)
            across(a, le).start()

    def give_back(a, i):
        return pltpu.make_async_remote_copy(
            src_ref=slab.at[a, slab_rows(peer(i))],
            dst_ref=back.at[a, slab_rows(me)],
            send_sem=bk_s.at[a, i], recv_sem=bk_r.at[a, i],
            device_id=(d, peer(i)), device_id_type=MESH,
        )

    def got_back(a, i):
        return pltpu.make_async_remote_copy(
            src_ref=slab.at[a, slab_rows(peer(i))],
            dst_ref=back.at[a, slab_rows(origin(i))],
            send_sem=bk_s.at[a, i], recv_sem=bk_r.at[a, i],
            device_id=(d, peer(i)), device_id_type=MESH,
        )

    def reduce_near(a):
        to_core(a, 0).wait_recv()
        totals = []
        for le in range(2):
            across(a, le).wait_recv()
            r = pl.ds(le * ROWS, ROWS)
            total = part[a, 0, 0, r, :].astype(F32) + crecv[a, 0, r, :].astype(F32)
            totals.append((total + zrecv[a, le].astype(F32)).astype(BF16))
        both = jnp.concatenate(totals, 0)
        slab[a, :, 0:WIDE] = dg(ungrp[0], both, 1, 0).astype(BF16)
        folded = jnp.zeros((256, GROUP), F32)
        for k in range(3):
            folded += dg(ungrp[1 + k], both[:, k * GROUP : (k + 1) * GROUP], 1, 0)
        slab[a, :, WIDE:MSG] = folded.astype(BF16)
        back[a, slab_rows(me), :] = slab[a, slab_rows(me), :]
        loop(1, 16, lambda i: give_back(a, i).start())

    def block_owner(k):
        return (4 * c + k // 2) * 2 + k % 2

    def hand_out(a, k):
        return pltpu.make_async_remote_copy(
            src_ref=blocks.at[a, k], dst_ref=frecv.at[a, z],
            send_sem=fb_s.at[a, k], recv_sem=fb_r.at[a, z],
            device_id=(block_owner(k), me), device_id_type=MESH,
        )

    def handed(a, zz):
        return pltpu.make_async_remote_copy(
            src_ref=blocks.at[a, 0], dst_ref=frecv.at[a, zz],
            send_sem=fb_s.at[a, 0], recv_sem=fb_r.at[a, zz],
            device_id=sib, device_id_type=MESH,
        )

    def tell(i):
        return pltpu.make_async_remote_copy(
            src_ref=dots.at[d], dst_ref=dots.at[d],
            send_sem=dt_s.at[i], recv_sem=dt_r.at[i],
            device_id=(lax.rem(d + i, 16), me), device_id_type=MESH,
        )

    def told(i):
        return pltpu.make_async_remote_copy(
            src_ref=dots.at[d], dst_ref=dots.at[lax.rem(d + 16 - i, 16)],
            send_sem=dt_s.at[i], recv_sem=dt_r.at[i],
            device_id=(lax.rem(d + i, 16), me), device_id_type=MESH,
        )

    def combine(a):
        loop(1, 16, lambda i: got_back(a, i).wait_recv())
        if a == 1:
            main_dot = back[1, :, HALF : HALF + 1].astype(F32)
            fold_dot = back[1, :, HALF + GROUP : HALF + GROUP + 1].astype(F32)
            main_dot = jnp.where(comb_one[0].astype(F32) > 0.5, main_dot, 0.0)
            fold_dot = jnp.where(comb_one[3].astype(F32) > 0.5, fold_dot, 0.0)
            lines = []
            for p in range(4):
                mine_p = jnp.where(ids[p : p + 1, :] == main_expert, main_dot, 0.0)
                mine_p += jnp.where(ids[p : p + 1, :] == fold_expert, fold_dot, 0.0)
                lines.append(jnp.sum(mine_p, 0, keepdims=True))
            dots[d] = jnp.concatenate(lines + [jnp.zeros((4, TOK), F32)], 0)
            loop(1, 16, lambda i: tell(i).start())
        tables = (comb_hi, comb_lo) if a == 0 else (comb_one,)
        pieces = []
        for k in range(3):
            value = jnp.zeros((TOK, GROUP), F32)
            for table in tables:
                value += dg(table[0], back[a, :, k * GROUP : (k + 1) * GROUP], 0, 0)
                value += dg(table[1 + k], back[a, :, WIDE:MSG], 0, 0)
            pieces.append(value.astype(BF16))
        total = dg(blksel[...], jnp.concatenate(pieces, 1), 1, 1).astype(BF16)
        for k in range(8):
            blocks[a, k] = total[k * BROWS : (k + 1) * BROWS, :]

        def body(k):
            @pl.when(block_owner(k) != d)
            def _():
                hand_out(a, k).start()

            @pl.when(block_owner(k) == d)
            def _():
                frecv[a, z] = blocks[a, k]

        loop(0, 8, body)

    def sender(zz):
        return zz * 2 + z // 4

    def finish(a, out_ref):
        def body(zz):
            @pl.when(sender(zz) != d)
            def _():
                handed(a, zz).wait_recv()

        loop(0, 8, body)
        total = frecv[a, 0].astype(F32)
        for zz in range(1, 8):
            total += frecv[a, zz].astype(F32)
        out_ref[...] = total[0:BLK, :].astype(BF16)

    def store(o, le, n):
        out = (gg_hbm, gu_hbm, gd_hbm)[n]
        e = expert_of(o, le)
        return pltpu.make_async_copy(grads.at[n, e], out.at[e], out_sem.at[n, e])

    def weight_grads(o):
        def body(le):
            e = expert_of(o, le)
            r = of_expert(le)
            both = dg(rows[0, o, r, 0:D], ggu[o, r, :], 0, 0)
            grads[0, e] = both[:, 0:HID].astype(BF16)
            grads[1, e] = both[:, HID : 2 * HID].astype(BF16)
            grads[2, e] = dg(rows[1, o, r, 0:D], hid[o, r, :], 0, 0).astype(BF16)
            for n in range(3):
                store(o, le, n).start()

        loop(0, 2, body)

    first_hop(0, 0, 16)
    second_hop(0)
    for load in loads[2:]:
        load.wait()
    first_hop(1, 0, 6)
    forward(0)
    first_hop(1, 6, 11)
    forward(1)
    first_hop(1, 11, 16)
    reduce_far(0)
    second_hop(1)
    backward(0)
    reduce_near(0)
    backward(1)
    reduce_far(1)
    weight_grads(0)
    reduce_near(1)
    combine(0)
    weight_grads(1)
    combine(1)
    finish(0, mixed_ref)
    finish(1, igrad_ref)
    loop(1, 16, lambda i: told(i).wait_recv())
    total = dots[0]
    for k in range(1, 16):
        total += dots[k]
    dot = total[0:4, :]
    rgrad_ref[...] = dot - weights * jnp.sum(dot, 0, keepdims=True)

    def sent(i):
        tell(i).wait_send()
        for a in range(2):
            dispatch(a, i).wait_send()
            give_back(a, i).wait_send()

    loop(1, 16, sent)

    def passed(s):
        for a in range(2):
            along_z(a, s).wait_send()
            for o in range(2):
                to_sibling(a, o, s).wait_send()

    loop(0, 16, passed)
    for a in range(2):
        for o in range(2):
            to_core(a, o).wait_send()
            across(a, o).wait_send()

        def out_block(k, a=a):
            @pl.when(block_owner(k) != d)
            def _():
                hand_out(a, k).wait_send()

        loop(0, 8, out_block)
    for o in range(2):
        for le in range(2):
            for n in range(3):
                store(o, le, n).wait()


def on_device(tokens, output_grad, router_logits, expert_ids, w_gate, w_up, w_down):
    anywhere = pl.BlockSpec(memory_space=pl.ANY)
    vmem = pl.BlockSpec(memory_space=pltpu.VMEM)
    dma = pltpu.SemaphoreType.DMA
    weight = jax.ShapeDtypeStruct((4, D, HID), BF16)
    block = jax.ShapeDtypeStruct((BLK, TOK), BF16)
    mixed, igrad, rgrad, gg, gu, gd = pl.pallas_call(
        kernel,
        out_shape=(block, block, jax.ShapeDtypeStruct((4, TOK), F32), weight, weight, weight),
        in_specs=[anywhere, anywhere, vmem, vmem, anywhere, anywhere, anywhere],
        out_specs=(vmem, vmem, vmem, anywhere, anywhere, anywhere),
        scratch_shapes=[
            pltpu.VMEM((PADDED, TOK), BF16),
            pltpu.VMEM((PADDED, TOK), BF16),
            pltpu.VMEM((4, D + WIDE - HALF, HID), BF16),
            pltpu.VMEM((4, D + WIDE - HALF, HID), BF16),
            pltpu.VMEM((4, D + WIDE - HALF, HID), BF16),
            pltpu.VMEM((2, 256, MSG), BF16),
            pltpu.VMEM((2, 2, 2, 256, MSG), BF16),
            pltpu.VMEM((2, 2, PAIR, PADDED), BF16),
            pltpu.VMEM((256, TOK), BF16),
            pltpu.VMEM((256, 3 * TOK), BF16),
            pltpu.VMEM((4, 256, TOK), BF16),
            pltpu.VMEM((4, 256, TOK), BF16),
            pltpu.VMEM((4, 256, TOK), BF16),
            pltpu.VMEM((4, PAIR, 256), BF16),
            pltpu.VMEM((4, 256, PAIR), BF16),
            pltpu.VMEM((8 * BROWS, WIDE), BF16),
            pltpu.VMEM((2, PAIR, HID), F32),
            pltpu.VMEM((2, PAIR, HID), F32),
            pltpu.VMEM((2, PAIR, HID), F32),
            pltpu.VMEM((2, PAIR, HID), F32),
            pltpu.VMEM((2, PAIR, HID), BF16),
            pltpu.VMEM((2, PAIR, 2 * HID), BF16),
            pltpu.VMEM((2, 2, 2, PAIR, WIDE), BF16),
            pltpu.VMEM((2, 2, PAIR, WIDE), BF16),
            pltpu.VMEM((2, 2, ROWS, WIDE), BF16),
            pltpu.VMEM((2, 2, ROWS, WIDE), BF16),
            pltpu.VMEM((2, 256, MSG), BF16),
            pltpu.VMEM((2, 256, MSG), BF16),
            pltpu.VMEM((2, 8, BROWS, TOK), BF16),
            pltpu.VMEM((2, 8, BROWS, TOK), BF16),
            pltpu.VMEM((16, 8, TOK), F32),
            pltpu.VMEM((3, 4, D, HID), BF16),
            dma((14,)),
            dma((2, 16)), dma((2, 16)),
            dma((2, 16)), dma((2, 16)),
            dma((2, 2, 16)), dma((2, 2, 16)),
            dma((2, 2)), dma((2, 2)),
            dma((2, 2)), dma((2, 2)),
            dma((2, 16)), dma((2, 16)),
            dma((2, 8)), dma((2, 8)),
            dma((16,)), dma((16,)),
            dma((3, 4)),
        ],
        compiler_params=pltpu.CompilerParams(
            collective_id=0, has_side_effects=True, vmem_limit_bytes=56 * 2**20
        ),
        cost_estimate=pl.CostEstimate(
            flops=2 * 9 * 640 * D * HID, bytes_accessed=9 * 10**6, transcendentals=640 * HID
        ),
        name="moe_layer",
    )(
        tokens.T, output_grad.T, router_logits.T, expert_ids.T,
        w_gate, w_up, jnp.swapaxes(w_down, 1, 2),
    )
    return mixed.T, igrad.T, rgrad.T, gg, gu, jnp.swapaxes(gd, 1, 2)


def solution(mesh):
    in_specs = (
        P("expert", None),
        P("expert", None),
        P("expert", None),
        P("expert", None),
        P("expert", None, "dp"),
        P("expert", None, "dp"),
        P("expert", "dp", None),
    )
    out_specs = (
        P("expert", "dp"),
        P("expert", "dp"),
        P("expert", None),
        P("expert", None, "dp"),
        P("expert", None, "dp"),
        P("expert", "dp", None),
    )
    return jax.shard_map(
        on_device, mesh=mesh, in_specs=in_specs, out_specs=out_specs, check_vma=False
    )
```

time: 264 us -> 90.1 us (0.34)
  blocking collectives: 132 us -> 0 us
  Pallas kernels: 0 us -> 79.4 us
  local copies, waits for them, and re-layouts: 53.3 us -> 9.65 us
  matrix products: 24 us -> 0 us
  starting transfers between devices: 23.3 us -> 0 us
  waiting for transfers between devices: 19.8 us -> 0 us
  other arithmetic: 6.91 us -> 0 us
    unnamed x2 -> x0, blocking collectives: 132 us -> none
    pallas_call x0 -> x1, Pallas kernels: none -> 79.4 us  [on_device(): pl.pallas_call(kernel, out_shape=(block, block, jax.ShapeDtypeStruct((4,...]
    dot_general x8 -> x0, matrix products: 24 us -> none  [the longest x1 4.09 us: on_device(): jnp.einsum('secd,edf->secf', rows_recv, w_gate, preferred_element_type=jn...]
    all_to_all x4 -> x0, starting transfers between devices: 23.3 us -> none  [the longest x2 12.3 us: route_out(): lax.all_to_all(buffer, 'expert', split_axis=0, concat_axis=0, tiled=True)]
    all_to_all x4 -> x0, waiting for transfers between devices: 19.8 us -> none  [the longest x2 14.6 us: route_out(): lax.all_to_all(buffer, 'expert', split_axis=0, concat_axis=0, tiled=True)]
    reshape x6 -> x0, local copies, waits for them, and re-layouts: 18.4 us -> none  [the longest x2 9.15 us: on_device(): send_rows = padded_tokens[slot_table // top_picks].reshape(buffer_shape)]
    gather x4 -> x0, local copies, waits for them, and re-layouts: 10 us -> none  [the longest x1 3.68 us: on_device(): send_rows = padded_tokens[slot_table // top_picks].reshape(buffer_shape)]
    convert_element_type x7 -> x0, local copies, waits for them, and re-layouts: 9.43 us -> none  [the longest x2 5.06 us: on_device(): jnp.repeat(output_grad, top_picks, axis=0).astype(jnp.float32)]
  transfers between devices with their start and end apart: 4 -> 0, of which waited for: 3 -> 0; matrix products, arithmetic and copies ran while one was open for 18% -> 0% of each run, Pallas kernels for 0% -> 0%
where the time goes in v1:
time: 90.1 us; the launch traced here: 89.7 us
  Pallas kernels  79.4 us (88%)
  local copies, waits for them, and re-layouts  9.65 us (11%)
    pallas_call x1, Pallas kernels, on_device(): pl.pallas_call(kernel, out_shape=(block, block, jax.ShapeDtypeStruct((4,...  79.4 us
    unnamed x10, local copies, waits for them, and re-layouts  9.65 us

profile of v1, /device:TPU:1, one launch (start us, length us, event | category | flops | bytes accessed | tf_op | source)
XLA Modules:
  0.0 89.7 jit_solution(5701180248658989704)
XLA Ops:
  0.6 79.4 %moe_layer.1 = (bf16[90,128]{1,0:T(8,128)(2,1)}, bf16[90,128]{1,0:T(8,128)(2,1)}, f32[4,128]{1,0:T(4,128)}, bf16[4,1440,128]{2,1,0:T(8,128)(2,1)}, bf16[4,1440,1...) custom-call(bf16[1440,128]{1,0:T(8,128)(2,1)} %bitcast.14, bf16[1440,128]{1,0:T(8,128)(2,1)} %bitcast.15, ...), custom_call_target="tpu_custom_call" | custom-call | flops 2123366400 | bytes 9000000 | tf_op jit(solution)/shard_map/moe_layer/pallas_call | solution.py:539
  80.1 1.3 %copy.19 = bf16[128,90]{0,1:T(8,128)(2,1)} copy(bf16[128,90]{0,1:T(8,128)(2,1)} %bitcast.11) | data formatting | bytes 46080
  81.4 1.3 %copy.20 = bf16[128,90]{0,1:T(8,128)(2,1)} copy(bf16[128,90]{0,1:T(8,128)(2,1)} %bitcast.10) | data formatting | bytes 46080
  82.8 1.2 %copy.21 = f32[128,4]{0,1:T(4,128)} copy(f32[128,4]{0,1:T(4,128)} %bitcast.12) | data formatting | bytes 4096
  84.0 0.0 copy-start.1
  84.0 2.7 %copy.22 = bf16[4,1440,128]{2,1,0:T(8,128)(2,1)} copy(bf16[4,1440,128]{2,1,0:T(8,128)(2,1)} %get-tuple-element.27) | data formatting | bytes 2949120
  86.7 0.0 copy-done.1
  86.7 0.0 copy-start
  86.7 1.1 %copy.23 = bf16[4,1440,128]{2,1,0:T(8,128)(2,1)} copy(bf16[4,1440,128]{2,1,0:T(8,128)(2,1)S(1)} %copy-done.1) | data formatting | bytes 2949120
  87.8 0.8 copy-done
  88.6 1.1 %copy.24 = bf16[4,128,1440]{1,2,0:T(8,128)(2,1)} copy(bf16[4,128,1440]{1,2,0:T(8,128)(2,1)S(1)} %bitcast.9) | data formatting | bytes 2949120
Async XLA Ops:
  84.0 2.7 %copy-start.1 = (bf16[4,1440,128]{2,1,0:T(8,128)(2,1)S(1)}, bf16[4,1440,128]{2,1,0:T(8,128)(2,1)}, u32[]{:S(2)}) copy-start(bf16[4,1440,128]{2,1,0:T(8,128)(2,1)} %get-tuple-element.28) | copy-start | bytes 4423684
  86.7 1.9 %copy-start = (bf16[4,1440,128]{2,1,0:T(8,128)(2,1)S(1)}, bf16[4,1440,128]{2,1,0:T(8,128)(2,1)}, u32[]{:S(2)}) copy-start(bf16[4,1440,128]{2,1,0:T(8,128)(2,1)} %get-tuple-element.17) | copy-start | bytes 4423684

commit v2 on v1

v2 whole, which is shorter than its diff:
```python
import jax
import jax.numpy as jnp
import numpy as np
from jax import lax
from jax.experimental import pallas as pl
from jax.experimental.pallas import tpu as pltpu
from jax.sharding import PartitionSpec as P

MESH = pl.DeviceIdType.MESH
F32 = jnp.float32
BF16 = jnp.bfloat16

D = 1440
HALF = 720
WIDE = 768
PADDED = 1536
HID = 128
TOK = 128
RANKS = 10
SRC = 16
ROWS = SRC * RANKS
PAIR = 2 * ROWS
SLAB = 16
MSG = 1024
GROUP = 256
PART = 384
STEP = 352
BACK = 512
DOT_LANE = 376
ORDER = (1, 12, 3, 4, 2, 8, 5, 15, 7, 13, 6, 14, 9, 11, 10)
FIRST = int(np.int32(np.uint32(sum(i << (4 * j) for j, i in enumerate(ORDER[:8])))))
LAST = sum(i << (4 * j) for j, i in enumerate(ORDER[8:]))
BLK = 90
BROWS = 96


def dg(a, b, ca, cb):
    return lax.dot_general(a, b, (((ca,), (cb,)), ((), ())), preferred_element_type=F32)


def iota(shape, dim):
    return lax.broadcasted_iota(jnp.int32, shape, dim)


def ones_where(mask):
    return jnp.where(mask, 1.0, 0.0).astype(BF16)


def kernel(
    tok_hbm, og_hbm, logits_ref, ids_ref, wg_hbm, wu_hbm, wd_hbm,
    mixed_ref, igrad_ref, rgrad_ref, gg_hbm, gu_hbm, gd_hbm,
    tok, og, wgu, wd,
    send_slab, cat, rows, sel_main, sel_fold, comb_hi, comb_lo, comb_one,
    grp, ungrp, blksel,
    sig, pre, act, upp, hid, ggu, dotc,
    part, crecv, zsend, zrecv, slab, back, blocks, frecv, dots,
    grads,
    in_sem, xy_s, xy_r, zf_s, zf_r, cf_s, cf_r, rc_s, rc_r, rz_s, rz_r,
    bk_s, bk_r, fb_s, fb_r, dt_s, dt_r, out_sem,
):
    d = lax.axis_index("dp")
    me = lax.axis_index("expert")
    z, c = lax.div(d, 2), lax.rem(d, 2)
    x, y = lax.div(me, 4), lax.rem(me, 4)
    par = lax.rem(z, 2)
    sib = (z * 2 + 1 - c, me)
    up = (lax.rem(z + 1, 8) * 2 + c, me)
    down = (lax.rem(z + 7, 8) * 2 + c, me)

    def peer(i):
        return lax.rem(x + i // 4, 4) * 4 + lax.rem(y + i % 4, 4)

    def origin(i):
        return lax.rem(x + 4 - i // 4, 4) * 4 + lax.rem(y + 4 - i % 4, 4)

    def slab_rows(s):
        return pl.ds(pl.multiple_of(s * SLAB, SLAB), SLAB)

    barrier = pltpu.get_barrier_semaphore()

    def greet(i, carry):
        pl.semaphore_signal(barrier, inc=1, device_id=(d, peer(i)), device_id_type=MESH)
        pl.semaphore_signal(
            barrier, inc=1, device_id=(lax.rem(d + i, 16), me), device_id_type=MESH
        )
        return carry

    lax.fori_loop(1, 16, greet, 0)

    loads = [
        pltpu.make_async_copy(tok_hbm, tok.at[pl.ds(0, D)], in_sem.at[0]),
        pltpu.make_async_copy(og_hbm, og.at[pl.ds(0, D)], in_sem.at[1]),
    ]
    for e in range(4):
        for n, src, dst in (
            (2, wg_hbm, wgu.at[e, pl.ds(0, D), pl.ds(0, HID)]),
            (2, wu_hbm, wgu.at[e, pl.ds(0, D), pl.ds(HID, HID)]),
            (3, wd_hbm, wd.at[e, pl.ds(0, D)]),
        ):
            loads.append(pltpu.make_async_copy(src.at[e], dst, in_sem.at[n]))
    loads[0].start()
    loads[1].start()
    tok[pl.ds(D, PADDED - D), :] = jnp.zeros((PADDED - D, TOK), BF16)
    og[pl.ds(D, PADDED - D), :] = jnp.zeros((PADDED - D, TOK), BF16)

    lifted = jnp.exp(logits_ref[...])
    weights = lifted / jnp.sum(lifted, 0, keepdims=True)
    ids = ids_ref[...]
    row = iota((256, TOK), 0)
    spot = row & 15
    earlier = ones_where(iota((TOK, TOK), 0) < iota((TOK, TOK), 1))

    def select(expert, rank):
        named = jnp.zeros((256, TOK), F32)
        weigh = jnp.zeros((256, TOK), F32)
        for p in range(4):
            same = ids[p : p + 1, :] == expert
            named = jnp.where(same, 1.0, named)
            weigh = jnp.where(same, weights[p : p + 1, :], weigh)
        before = dg(named.astype(BF16), earlier, 1, 0)
        chosen = (before == rank.astype(F32)) & (named > 0.5)
        return chosen, jnp.where(chosen, weigh, 0.0)

    second = jnp.where(spot >= RANKS, 1, 0)
    base = 4 * (row >> 4) + 2 * par
    main_expert = base + second
    fold_expert = base + 1
    main, main_w = select(main_expert, spot - RANKS * second)
    fold, fold_w = select(fold_expert, 6 + (spot & 3))
    sel_main[...] = ones_where(main)
    for k in range(3):
        sel_fold[:, k * TOK : (k + 1) * TOK] = ones_where(fold & ((spot >> 2) == k))
    start = pl.multiple_of(c * WIDE, WIDE)

    def gather(a, source):
        loads[a].wait()
        whole = dg(sel_main[...], source[pl.ds(start, WIDE), :], 1, 1)
        folded = jnp.zeros((256, GROUP), F32)
        for k in range(3):
            feats = source[pl.ds(pl.multiple_of(start + k * GROUP, GROUP), GROUP), :]
            folded += dg(sel_fold[:, k * TOK : (k + 1) * TOK], feats, 1, 1)
        if a == 1:
            whole = jnp.sum(main_w, 1, keepdims=True) * whole
            some = jnp.where((spot >> 2) < 3, fold_w, 0.0)
            folded = jnp.sum(some, 1, keepdims=True) * folded
        send_slab[a, :, 0:WIDE] = whole.astype(BF16)
        send_slab[a, :, WIDE:MSG] = folded.astype(BF16)

    def dispatch(a, i):
        return pltpu.make_async_remote_copy(
            src_ref=send_slab.at[a, slab_rows(peer(i))],
            dst_ref=cat.at[a, 0, c, slab_rows(me)],
            send_sem=xy_s.at[a], recv_sem=xy_r.at[a, i],
            device_id=(d, peer(i)), device_id_type=MESH,
        )

    def arrive(a, i):
        return pltpu.make_async_remote_copy(
            src_ref=send_slab.at[a, slab_rows(peer(i))],
            dst_ref=cat.at[a, 0, c, slab_rows(origin(i))],
            send_sem=xy_s.at[a], recv_sem=xy_r.at[a, i],
            device_id=(d, peer(i)), device_id_type=MESH,
        )

    def along_z(a, s):
        side = s // 8
        return pltpu.make_async_remote_copy(
            src_ref=cat.at[a, 0, c, slab_rows(s)],
            dst_ref=cat.at[a, 1, c, slab_rows(s)],
            send_sem=zf_s.at[a], recv_sem=zf_r.at[a, side],
            device_id=(lax.rem(z + 1 - 2 * side + 8, 8) * 2 + c, me), device_id_type=MESH,
        )

    def along_z_all(a, side):
        eight = pl.ds(8 * SLAB * side, 8 * SLAB)
        return pltpu.make_async_remote_copy(
            src_ref=cat.at[a, 0, c, eight], dst_ref=cat.at[a, 1, c, eight],
            send_sem=zf_s.at[a], recv_sem=zf_r.at[a, side],
            device_id=down if side else up, device_id_type=MESH,
        )

    def to_sibling(a, o, s, count=1):
        some = pl.ds(pl.multiple_of(s * SLAB, SLAB), count * SLAB)
        return pltpu.make_async_remote_copy(
            src_ref=cat.at[a, o, c, some], dst_ref=cat.at[a, o, c, some],
            send_sem=cf_s.at[a, o], recv_sem=cf_r.at[a, o],
            device_id=sib, device_id_type=MESH,
        )

    def from_sibling(a, o):
        return pltpu.make_async_remote_copy(
            src_ref=cat.at[a, o, c], dst_ref=cat.at[a, o, 1 - c],
            send_sem=cf_s.at[a, o], recv_sem=cf_r.at[a, o],
            device_id=sib, device_id_type=MESH,
        )

    def loop(lo, hi, body):
        def step(i, carry):
            body(i)
            return carry

        lax.fori_loop(lo, hi, step, 0)

    def turn(j):
        return (jnp.where(j < 8, FIRST, LAST) >> (4 * lax.rem(j, 8))) & 15

    gather(0, tok)
    pl.semaphore_wait(barrier, 30)
    loop(0, 15, lambda j: dispatch(0, turn(j)).start())
    cat[0, 0, c, slab_rows(me), :] = send_slab[0, slab_rows(me), :]
    along_z(0, me).start()
    to_sibling(0, 0, me).start()
    for load in loads[2:]:
        load.start()
    gather(1, og)
    cat[1, 0, c, slab_rows(me), :] = send_slab[1, slab_rows(me), :]

    for e in range(4):
        wgu[e, pl.ds(D, WIDE - HALF), :] = jnp.zeros((WIDE - HALF, 2 * HID), BF16)
        wd[e, pl.ds(D, WIDE - HALF), :] = jnp.zeros((WIDE - HALF, HID), BF16)
    comb_hi[0] = main_w.astype(BF16)
    comb_lo[0] = (main_w - main_w.astype(BF16).astype(F32)).astype(BF16)
    comb_one[0] = sel_main[...]
    for k in range(3):
        here = (spot >> 2) == k
        w_here = jnp.where(here, fold_w, 0.0)
        comb_hi[1 + k] = w_here.astype(BF16)
        comb_lo[1 + k] = (w_here - w_here.astype(BF16).astype(F32)).astype(BF16)
        comb_one[1 + k] = sel_fold[:, k * TOK : (k + 1) * TOK]

    n = iota((PAIR, 256), 0)
    i = iota((PAIR, 256), 1)
    later = jnp.where(n >= ROWS, 1, 0)
    m = n - ROWS * later
    s = (m * 6554) >> 16
    q = m - RANKS * s + RANKS * later
    grp[0] = ones_where((i == s * SLAB + q) & (q < 16))
    for k in range(3):
        grp[1 + k] = ones_where((i == s * SLAB + 4 * k + q - 16) & (q >= 16))
    n = iota((256, PAIR), 1)
    i = iota((256, PAIR), 0)
    later = jnp.where(n >= ROWS, 1, 0)
    m = n - ROWS * later
    s = (m * 6554) >> 16
    q = m - RANKS * s + RANKS * later
    ungrp[0] = ones_where((i == s * SLAB + q) & (q < 16))
    for k in range(3):
        ungrp[1 + k] = ones_where((i == s * SLAB + 4 * k + q - 16) & (q >= 16))
    line = iota((4 * BROWS, PART), 0)
    block = (line * 683) >> 16
    inner = line - BROWS * block
    place = BLK * block + inner
    for f in range(2):
        blksel[f] = ones_where((iota((4 * BROWS, PART), 1) == place + 8 * f) & (inner < BLK))

    def first_hop(a, lo, hi):
        def body(j):
            i = turn(j)
            arrive(a, i).wait_recv()

            along_z(a, origin(i)).start()
            to_sibling(a, 0, origin(i)).start()
            if a == 0:
                dispatch(1, i).start()

        loop(lo, hi, body)

    def second_hop(a):
        for side in range(2):
            along_z_all(a, side).wait_recv()
            to_sibling(a, 1, 8 * side, 8).start()

    def regroup(a, o):
        from_sibling(a, o).wait_recv()
        for h in range(2):
            folded = cat[a, o, h, :, WIDE:MSG]
            for k in range(3):
                value = dg(grp[0], cat[a, o, h, :, k * GROUP : (k + 1) * GROUP], 1, 0)
                value += dg(grp[1 + k], folded, 1, 0)
                rows[a, o, :, h * WIDE + k * GROUP : h * WIDE + (k + 1) * GROUP] = value.astype(BF16)

    def expert_of(o, le):
        return 2 * (par + o - 2 * par * o) + le

    def of_expert(le):
        return pl.ds(pl.multiple_of(le * ROWS, ROWS), ROWS)

    def feats(far, f):
        side = 1 - c if far else c
        return pl.ds(pl.multiple_of(side * HALF + f * STEP, 16), PART)

    def to_core(a, f, o):
        return pltpu.make_async_remote_copy(
            src_ref=part.at[a, 1, f, o], dst_ref=crecv.at[a, f, o],
            send_sem=rc_s.at[a], recv_sem=rc_r.at[a, f, o],
            device_id=sib, device_id_type=MESH,
        )

    def forward(o):
        regroup(0, o)

        def body(le):
            e = expert_of(o, le)
            r = of_expert(le)
            xe = rows[0, o, r, 0:D]
            both = dg(xe, wgu[e, pl.ds(0, D), :], 1, 0)
            pg = both[:, 0:HID]
            pu = both[:, HID : 2 * HID] + 1.0
            sg = jax.nn.sigmoid(1.702 * pg)
            ac = pg * sg
            sig[o, r, :] = sg
            pre[o, r, :] = pg
            act[o, r, :] = ac
            upp[o, r, :] = pu
            hid[o, r, :] = (ac * pu).astype(BF16)

        loop(0, 2, body)

    def outputs(o, f):
        def body(le):
            e = expert_of(o, le)
            r = of_expert(le)
            for far in range(2):
                value = dg(hid[o, r, :], wd[e, feats(far, f), :], 1, 1)
                part[0, far, f, o, r, :] = value.astype(BF16)

        loop(0, 2, body)
        to_core(0, f, o).start()

    def backward(o):
        regroup(1, o)

        def body(le):
            e = expert_of(o, le)
            r = of_expert(le)
            ge = rows[1, o, r, 0:D]
            hg = dg(ge, wd[e, pl.ds(0, D), :], 1, 0)
            sg, pg, ac, pu = sig[o, r, :], pre[o, r, :], act[o, r, :], upp[o, r, :]
            slope = sg + 1.702 * pg * sg * (1.0 - sg)
            ggu[o, r, 0:HID] = (hg * pu * slope).astype(BF16)
            ggu[o, r, HID : 2 * HID] = (hg * ac).astype(BF16)
            dot = jnp.sum(hid[o, r, :].astype(F32) * hg, 1, keepdims=True)
            dotc[o, r, :] = jnp.broadcast_to(dot, (ROWS, HID))

        loop(0, 2, body)

    def inputs(o, f):
        def body(le):
            e = expert_of(o, le)
            r = of_expert(le)
            for far in range(2):
                value = dg(ggu[o, r, :], wgu[e, feats(far, f), :], 1, 1)
                if f == 1:
                    dot = dotc[o, r, 0:1] if far == 0 else 0.0
                    value = jnp.where(iota((ROWS, PART), 1) == DOT_LANE, dot, value)
                part[1, far, f, o, r, :] = value.astype(BF16)

        loop(0, 2, body)
        to_core(1, f, o).start()

    def across(a, f, le):
        return pltpu.make_async_remote_copy(
            src_ref=zsend.at[a, f, le], dst_ref=zrecv.at[a, f, le],
            send_sem=rz_s.at[a], recv_sem=rz_r.at[a, f],
            device_id=up if le == 0 else down, device_id_type=MESH,
        )

    def reduce_far(a, f):
        to_core(a, f, 1).wait_recv()
        for le in range(2):
            r = pl.ds(le * ROWS, ROWS)
            total = part[a, 0, f, 1, r, :].astype(F32) + crecv[a, f, 1, r, :].astype(F32)
            zsend[a, f, le] = total.astype(BF16)
            across(a, f, le).start()

    def give_back(a, f, i):
        return pltpu.make_async_remote_copy(
            src_ref=slab.at[a, f, slab_rows(peer(i))],
            dst_ref=back.at[a, f, slab_rows(me)],
            send_sem=bk_s.at[a, f], recv_sem=bk_r.at[a, f],
            device_id=(d, peer(i)), device_id_type=MESH,
        )

    def all_back(a, f):
        fifteen = pl.ds(0, 15 * SLAB)
        return pltpu.make_async_remote_copy(
            src_ref=slab.at[a, f, fifteen], dst_ref=back.at[a, f, fifteen],
            send_sem=bk_s.at[a, f], recv_sem=bk_r.at[a, f],
            device_id=sib, device_id_type=MESH,
        )

    def reduce_near(a, f):
        to_core(a, f, 0).wait_recv()
        totals = []
        pltpu.make_async_remote_copy(
            src_ref=zsend.at[a, f], dst_ref=zrecv.at[a, f],
            send_sem=rz_s.at[a], recv_sem=rz_r.at[a, f],
            device_id=up, device_id_type=MESH,
        ).wait_recv()
        for le in range(2):
            r = pl.ds(le * ROWS, ROWS)
            total = part[a, 0, f, 0, r, :].astype(F32) + crecv[a, f, 0, r, :].astype(F32)
            totals.append((total + zrecv[a, f, le].astype(F32)).astype(BF16))
        both = jnp.concatenate(totals, 0)
        slab[a, f, :, 0:PART] = dg(ungrp[0], both, 1, 0).astype(BF16)
        folded = jnp.zeros((256, TOK), F32)
        for k in range(3):
            folded += dg(ungrp[1 + k], both[:, k * TOK : (k + 1) * TOK], 1, 0)
        slab[a, f, :, PART:BACK] = folded.astype(BF16)
        back[a, f, slab_rows(me), :] = slab[a, f, slab_rows(me), :]
        loop(1, 16, lambda i: give_back(a, f, i).start())

    def block_owner(k):
        return (4 * c + k // 2) * 2 + k % 2

    def hand_out(a, k):
        return pltpu.make_async_remote_copy(
            src_ref=blocks.at[a, k], dst_ref=frecv.at[a, z],
            send_sem=fb_s.at[a], recv_sem=fb_r.at[a],
            device_id=(block_owner(k), me), device_id_type=MESH,
        )

    def handed(a, count):
        return pltpu.make_async_remote_copy(
            src_ref=blocks.at[a, pl.ds(0, count)], dst_ref=frecv.at[a, pl.ds(0, count)],
            send_sem=fb_s.at[a], recv_sem=fb_r.at[a],
            device_id=sib, device_id_type=MESH,
        )

    def tell(i):
        return pltpu.make_async_remote_copy(
            src_ref=dots.at[d], dst_ref=dots.at[d],
            send_sem=dt_s, recv_sem=dt_r,
            device_id=(lax.rem(d + i, 16), me), device_id_type=MESH,
        )

    def told():
        return pltpu.make_async_remote_copy(
            src_ref=dots.at[pl.ds(0, 15)], dst_ref=dots.at[pl.ds(0, 15)],
            send_sem=dt_s, recv_sem=dt_r,
            device_id=sib, device_id_type=MESH,
        )

    def combine(a, f):
        all_back(a, f).wait_recv()
        if a == 1 and f == 1:
            main_dot = back[1, 1, :, DOT_LANE : DOT_LANE + 1].astype(F32)
            lane = DOT_LANE + TOK
            fold_dot = back[1, 1, :, lane : lane + 1].astype(F32)
            main_dot = jnp.where(comb_one[0].astype(F32) > 0.5, main_dot, 0.0)
            fold_dot = jnp.where(comb_one[3].astype(F32) > 0.5, fold_dot, 0.0)
            lines = []
            for p in range(4):
                mine_p = jnp.where(ids[p : p + 1, :] == main_expert, main_dot, 0.0)
                mine_p += jnp.where(ids[p : p + 1, :] == fold_expert, fold_dot, 0.0)
                lines.append(jnp.sum(mine_p, 0, keepdims=True))
            dots[d] = jnp.concatenate(lines + [jnp.zeros((4, TOK), F32)], 0)
            loop(1, 16, lambda i: tell(i).start())
        tables = (comb_hi, comb_lo) if a == 0 else (comb_one,)
        value = jnp.zeros((TOK, PART), F32)
        for table in tables:
            value += dg(table[0], back[a, f, :, 0:PART], 0, 0)
            value += jnp.concatenate(
                [dg(table[1 + k], back[a, f, :, PART:BACK], 0, 0) for k in range(3)], 1
            )
        total = dg(blksel[f], value.astype(BF16), 1, 1).astype(BF16)
        for k in range(4):
            blocks[a, 4 * f + k] = total[k * BROWS : (k + 1) * BROWS, :]

        def body(k):
            @pl.when(block_owner(k) != d)
            def _():
                hand_out(a, k).start()

            @pl.when(block_owner(k) == d)
            def _():
                frecv[a, z] = blocks[a, k]

        loop(4 * f, 4 * f + 4, body)

    inside = lax.div(z, 4) == c

    def finish(a, out_ref):
        @pl.when(inside)
        def _():
            handed(a, 7).wait_recv()

        @pl.when(jnp.logical_not(inside))
        def _():
            handed(a, 8).wait_recv()

        total = frecv[a, 0].astype(F32)
        for zz in range(1, 8):
            total += frecv[a, zz].astype(F32)
        out_ref[...] = total[0:BLK, :].astype(BF16)

    def store(o, le, n):
        out = (gg_hbm, gu_hbm, gd_hbm)[n]
        e = expert_of(o, le)
        return pltpu.make_async_copy(grads.at[n, e], out.at[e], out_sem.at[n])

    def weight_grads(o):
        def body(le):
            e = expert_of(o, le)
            r = of_expert(le)
            both = dg(rows[0, o, r, 0:D], ggu[o, r, :], 0, 0)
            grads[0, e] = both[:, 0:HID].astype(BF16)
            grads[1, e] = both[:, HID : 2 * HID].astype(BF16)
            grads[2, e] = dg(rows[1, o, r, 0:D], hid[o, r, :], 0, 0).astype(BF16)
            for n in range(3):
                store(o, le, n).start()

        loop(0, 2, body)

    first_hop(0, 0, 15)
    along_z(1, me).start()
    to_sibling(1, 0, me).start()
    for n, w in ((2, wgu), (3, wd)):
        all_rows = w.at[:, pl.ds(0, D)]
        pltpu.make_async_copy(all_rows, all_rows, in_sem.at[n]).wait()
    forward(0)
    outputs(0, 0)
    outputs(0, 1)
    second_hop(0)
    first_hop(1, 0, 8)
    forward(1)
    outputs(1, 0)
    outputs(1, 1)
    first_hop(1, 8, 15)
    reduce_far(0, 0)
    reduce_far(0, 1)
    backward(0)
    second_hop(1)
    reduce_near(0, 0)
    reduce_near(0, 1)
    backward(1)
    for f in range(2):
        inputs(1, f)
        inputs(0, f)
    reduce_far(1, 0)
    reduce_far(1, 1)
    weight_grads(0)
    reduce_near(1, 0)
    reduce_near(1, 1)
    combine(0, 0)
    combine(0, 1)
    weight_grads(1)
    combine(1, 0)
    combine(1, 1)
    finish(0, mixed_ref)
    finish(1, igrad_ref)
    told().wait_recv()
    total = dots[0]
    for k in range(1, 16):
        total += dots[k]
    dot = total[0:4, :]
    rgrad_ref[...] = dot - weights * jnp.sum(dot, 0, keepdims=True)

    told().wait_send()
    for a in range(2):
        fifteen = pl.ds(0, 15 * SLAB)
        pltpu.make_async_remote_copy(
            src_ref=send_slab.at[a, fifteen], dst_ref=cat.at[a, 0, c, fifteen],
            send_sem=xy_s.at[a], recv_sem=xy_r.at[a, 0],
            device_id=sib, device_id_type=MESH,
        ).wait_send()
        pltpu.make_async_remote_copy(
            src_ref=cat.at[a, 0, c], dst_ref=cat.at[a, 1, c],
            send_sem=zf_s.at[a], recv_sem=zf_r.at[a, 0],
            device_id=sib, device_id_type=MESH,
        ).wait_send()
        pltpu.make_async_remote_copy(
            src_ref=part.at[a, 1], dst_ref=crecv.at[a],
            send_sem=rc_s.at[a], recv_sem=rc_r.at[a, 0, 0],
            device_id=sib, device_id_type=MESH,
        ).wait_send()
        pltpu.make_async_remote_copy(
            src_ref=zsend.at[a], dst_ref=zrecv.at[a],
            send_sem=rz_s.at[a], recv_sem=rz_r.at[a, 0],
            device_id=sib, device_id_type=MESH,
        ).wait_send()
        for f in range(2):
            from_sibling(a, f).wait_send()
            all_back(a, f).wait_send()

        @pl.when(inside)
        def _():
            handed(a, 7).wait_send()

        @pl.when(jnp.logical_not(inside))
        def _():
            handed(a, 8).wait_send()

    for n, out in enumerate((gg_hbm, gu_hbm, gd_hbm)):
        pltpu.make_async_copy(grads.at[n], out, out_sem.at[n]).wait()


def deliver(mixed_in, igrad_in, rgrad_in, gg_in, gu_in, gd_in, *outs):
    for src, dst in zip((mixed_in, igrad_in, rgrad_in, gg_in, gu_in, gd_in), outs):
        dst[...] = src[...]


def on_device(tokens, output_grad, router_logits, expert_ids, w_gate, w_up, w_down):
    anywhere = pl.BlockSpec(memory_space=pl.ANY)
    vmem = pl.BlockSpec(memory_space=pltpu.VMEM)
    dma = pltpu.SemaphoreType.DMA
    weight = jax.ShapeDtypeStruct((4, D, HID), BF16)
    block = jax.ShapeDtypeStruct((BLK, TOK), BF16)
    mixed, igrad, rgrad, gg, gu, gd = pl.pallas_call(
        kernel,
        out_shape=(block, block, jax.ShapeDtypeStruct((4, TOK), F32), weight, weight, weight),
        in_specs=[anywhere, anywhere, vmem, vmem, anywhere, anywhere, anywhere],
        out_specs=(vmem, vmem, vmem, anywhere, anywhere, anywhere),
        scratch_shapes=[
            pltpu.VMEM((PADDED, TOK), BF16),
            pltpu.VMEM((PADDED, TOK), BF16),
            pltpu.VMEM((4, D + WIDE - HALF, 2 * HID), BF16),
            pltpu.VMEM((4, D + WIDE - HALF, HID), BF16),
            pltpu.VMEM((2, 256, MSG), BF16),
            pltpu.VMEM((2, 2, 2, 256, MSG), BF16),
            pltpu.VMEM((2, 2, PAIR, PADDED), BF16),
            pltpu.VMEM((256, TOK), BF16),
            pltpu.VMEM((256, 3 * TOK), BF16),
            pltpu.VMEM((4, 256, TOK), BF16),
            pltpu.VMEM((4, 256, TOK), BF16),
            pltpu.VMEM((4, 256, TOK), BF16),
            pltpu.VMEM((4, PAIR, 256), BF16),
            pltpu.VMEM((4, 256, PAIR), BF16),
            pltpu.VMEM((2, 4 * BROWS, PART), BF16),
            pltpu.VMEM((2, PAIR, HID), F32),
            pltpu.VMEM((2, PAIR, HID), F32),
            pltpu.VMEM((2, PAIR, HID), F32),
            pltpu.VMEM((2, PAIR, HID), F32),
            pltpu.VMEM((2, PAIR, HID), BF16),
            pltpu.VMEM((2, PAIR, 2 * HID), BF16),
            pltpu.VMEM((2, PAIR, HID), F32),
            pltpu.VMEM((2, 2, 2, 2, PAIR, PART), BF16),
            pltpu.VMEM((2, 2, 2, PAIR, PART), BF16),
            pltpu.VMEM((2, 2, 2, ROWS, PART), BF16),
            pltpu.VMEM((2, 2, 2, ROWS, PART), BF16),
            pltpu.VMEM((2, 2, 256, BACK), BF16),
            pltpu.VMEM((2, 2, 256, BACK), BF16),
            pltpu.VMEM((2, 8, BROWS, TOK), BF16),
            pltpu.VMEM((2, 8, BROWS, TOK), BF16),
            pltpu.VMEM((16, 8, TOK), F32),
            pltpu.VMEM((3, 4, D, HID), BF16),
            dma((4,)),
            dma((2,)), dma((2, 16)),
            dma((2,)), dma((2, 2)),
            dma((2, 2)), dma((2, 2)),
            dma((2,)), dma((2, 2, 2)),
            dma((2,)), dma((2, 2)),
            dma((2, 2)), dma((2, 2)),
            dma((2,)), dma((2,)),
            dma(()), dma(()),
            dma((3,)),
        ],
        compiler_params=pltpu.CompilerParams(
            collective_id=0, has_side_effects=True, vmem_limit_bytes=58 * 2**20
        ),
        cost_estimate=pl.CostEstimate(
            flops=2 * 9 * 640 * D * HID, bytes_accessed=9 * 10**6, transcendentals=640 * HID
        ),
        name="moe_layer",
    )(
        tokens.T, output_grad.T, router_logits.T, expert_ids.T,
        w_gate, w_up, jnp.swapaxes(w_down, 1, 2),
    )
    small = pl.BlockSpec((BLK, TOK), lambda e: (0, 0))
    tiny = pl.BlockSpec((4, TOK), lambda e: (0, 0))
    large = pl.BlockSpec((1, D, HID), lambda e: (e, 0, 0))
    mixed, igrad, rgrad, gg, gu, gd = pl.pallas_call(
        deliver,
        grid=(4,),
        out_shape=(block, block, jax.ShapeDtypeStruct((4, TOK), F32), weight, weight, weight),
        in_specs=[small, small, tiny, large, large, large],
        out_specs=(small, small, tiny, large, large, large),
        cost_estimate=pl.CostEstimate(flops=0, bytes_accessed=9 * 10**6, transcendentals=0),
        name="deliver",
    )(mixed, igrad, rgrad, gg, gu, gd)
    return mixed.T, igrad.T, rgrad.T, gg, gu, jnp.swapaxes(gd, 1, 2)


def solution(mesh):
    in_specs = (
        P("expert", None),
        P("expert", None),
        P("expert", None),
        P("expert", None),
        P("expert", None, "dp"),
        P("expert", None, "dp"),
        P("expert", "dp", None),
    )
    out_specs = (
        P("expert", "dp"),
        P("expert", "dp"),
        P("expert", None),
        P("expert", None, "dp"),
        P("expert", None, "dp"),
        P("expert", "dp", None),
    )
    return jax.shard_map(
        on_device, mesh=mesh, in_specs=in_specs, out_specs=out_specs, check_vma=False
    )
```

time: 90.1 us -> 73.3 us (0.81)
  local copies, waits for them, and re-layouts: 9.65 us -> 0 us
  Pallas kernels: 79.4 us -> 72.5 us
    pallas_call x1, Pallas kernels: 79.4 us -> 67.6 us  [on_device(): pl.pallas_call(kernel, out_shape=(block, block, jax.ShapeDtypeStruct((4,...]
    unnamed x10 -> x0, local copies, waits for them, and re-layouts: 9.65 us -> none
    pallas_call x0 -> x1, Pallas kernels: none -> 4.85 us  [on_device(): pl.pallas_call(deliver, grid=(4,), out_shape=(block, block, jax.ShapeDtyp...]
where the time goes in v2:
time: 73.3 us; the launch traced here: 73.1 us
  Pallas kernels  72.5 us (99%)
    pallas_call x1, Pallas kernels, on_device(): pl.pallas_call(kernel, out_shape=(block, block, jax.ShapeDtypeStruct((4,...  67.6 us
    pallas_call x1, Pallas kernels, on_device(): pl.pallas_call(deliver, grid=(4,), out_shape=(block, block, jax.ShapeDtyp...  4.85 us

profile of v2, /device:TPU:1, one launch (start us, length us, event | category | flops | bytes accessed | tf_op | source)
XLA Modules:
  0.0 73.1 jit_solution(334325699254954926)
XLA Ops:
  0.6 67.6 %moe_layer.1 = (bf16[90,128]{1,0:T(8,128)(2,1)}, bf16[90,128]{1,0:T(8,128)(2,1)}, f32[4,128]{1,0:T(4,128)}, bf16[4,1440,128]{2,1,0:T(8,128)(2,1)}, bf16[4,1440,1...) custom-call(bf16[1440,128]{1,0:T(8,128)(2,1)} %bitcast.11, bf16[1440,128]{1,0:T(8,128)(2,1)} %bitcast.12, ...), custom_call_target="tpu_custom_call" | custom-call | flops 2123366400 | bytes 9000000 | tf_op jit(solution)/shard_map/moe_layer/pallas_call | solution.py:609
  68.3 4.8 %deliver.1 = (bf16[90,128]{1,0:T(8,128)(2,1)}, bf16[90,128]{1,0:T(8,128)(2,1)}, f32[4,128]{1,0:T(4,128)}, bf16[4,1440,128]{2,1,0:T(8,128)(2,1)}, bf16[4,1440,128...) custom-call(bf16[90,128]{1,0:T(8,128)(2,1)} %get-tuple-element.18.mixed_in, bf16[90,128]{1,0:T(8,128)(2,1)} %get-tuple-element.19.igrad_in, ...), custom_call_target="tpu_custom_call" | custom-call | bytes 9000000 | tf_op jit(solution)/shard_map/deliver/pallas_call | solution.py:672

commit v3 on v2

--- a/solution.py
+++ b/solution.py
@@ -125,6 +125,9 @@
     base = 4 * (row >> 4) + 2 * par
     main_expert = base + second
     fold_expert = base + 1
+    base_back = 4 * (row >> 4) + 2 * (1 - par)
+    main_back = base_back + second
+    fold_back = base_back + 1
     main, main_w = select(main_expert, spot - RANKS * second)
     fold, fold_w = select(fold_expert, 6 + (spot & 3))
     sel_main[...] = ones_where(main)
@@ -218,15 +221,17 @@
     for e in range(4):
         wgu[e, pl.ds(D, WIDE - HALF), :] = jnp.zeros((WIDE - HALF, 2 * HID), BF16)
         wd[e, pl.ds(D, WIDE - HALF), :] = jnp.zeros((WIDE - HALF, HID), BF16)
+    main, main_w = select(main_back, spot - RANKS * second)
+    fold, fold_w = select(fold_back, 6 + (spot & 3))
     comb_hi[0] = main_w.astype(BF16)
     comb_lo[0] = (main_w - main_w.astype(BF16).astype(F32)).astype(BF16)
-    comb_one[0] = sel_main[...]
+    comb_one[0] = ones_where(main)
     for k in range(3):
         here = (spot >> 2) == k
         w_here = jnp.where(here, fold_w, 0.0)
         comb_hi[1 + k] = w_here.astype(BF16)
         comb_lo[1 + k] = (w_here - w_here.astype(BF16).astype(F32)).astype(BF16)
-        comb_one[1 + k] = sel_fold[:, k * TOK : (k + 1) * TOK]
+        comb_one[1 + k] = ones_where(fold & here)
 
     n = iota((PAIR, 256), 0)
     i = iota((PAIR, 256), 1)
@@ -260,8 +265,6 @@
 
             along_z(a, origin(i)).start()
             to_sibling(a, 0, origin(i)).start()
-            if a == 0:
-                dispatch(1, i).start()
 
         loop(lo, hi, body)
 
@@ -366,10 +369,10 @@
         )
 
     def reduce_far(a, f):
-        to_core(a, f, 1).wait_recv()
+        to_core(a, f, 0).wait_recv()
         for le in range(2):
             r = pl.ds(le * ROWS, ROWS)
-            total = part[a, 0, f, 1, r, :].astype(F32) + crecv[a, f, 1, r, :].astype(F32)
+            total = part[a, 0, f, 0, r, :].astype(F32) + crecv[a, f, 0, r, :].astype(F32)
             zsend[a, f, le] = total.astype(BF16)
             across(a, f, le).start()
 
@@ -390,7 +393,7 @@
         )
 
     def reduce_near(a, f):
-        to_core(a, f, 0).wait_recv()
+        to_core(a, f, 1).wait_recv()
         totals = []
         pltpu.make_async_remote_copy(
             src_ref=zsend.at[a, f], dst_ref=zrecv.at[a, f],
@@ -399,7 +402,7 @@
         ).wait_recv()
         for le in range(2):
             r = pl.ds(le * ROWS, ROWS)
-            total = part[a, 0, f, 0, r, :].astype(F32) + crecv[a, f, 0, r, :].astype(F32)
+            total = part[a, 0, f, 1, r, :].astype(F32) + crecv[a, f, 1, r, :].astype(F32)
             totals.append((total + zrecv[a, f, le].astype(F32)).astype(BF16))
         both = jnp.concatenate(totals, 0)
         slab[a, f, :, 0:PART] = dg(ungrp[0], both, 1, 0).astype(BF16)
@@ -451,8 +454,8 @@
             fold_dot = jnp.where(comb_one[3].astype(F32) > 0.5, fold_dot, 0.0)
             lines = []
             for p in range(4):
-                mine_p = jnp.where(ids[p : p + 1, :] == main_expert, main_dot, 0.0)
-                mine_p += jnp.where(ids[p : p + 1, :] == fold_expert, fold_dot, 0.0)
+                mine_p = jnp.where(ids[p : p + 1, :] == main_back, main_dot, 0.0)
+                mine_p += jnp.where(ids[p : p + 1, :] == fold_back, fold_dot, 0.0)
                 lines.append(jnp.sum(mine_p, 0, keepdims=True))
             dots[d] = jnp.concatenate(lines + [jnp.zeros((4, TOK), F32)], 0)
             loop(1, 16, lambda i: tell(i).start())
@@ -513,6 +516,7 @@
         loop(0, 2, body)
 
     first_hop(0, 0, 15)
+    loop(0, 15, lambda j: dispatch(1, turn(j)).start())
     along_z(1, me).start()
     to_sibling(1, 0, me).start()
     for n, w in ((2, wgu), (3, wd)):
@@ -522,24 +526,26 @@
     outputs(0, 0)
     outputs(0, 1)
     second_hop(0)
-    first_hop(1, 0, 8)
+    first_hop(1, 0, 5)
+    reduce_far(0, 0)
+    reduce_far(0, 1)
     forward(1)
+    first_hop(1, 5, 10)
     outputs(1, 0)
     outputs(1, 1)
-    first_hop(1, 8, 15)
-    reduce_far(0, 0)
-    reduce_far(0, 1)
+    first_hop(1, 10, 15)
     backward(0)
-    second_hop(1)
+    inputs(0, 0)
+    inputs(0, 1)
     reduce_near(0, 0)
     reduce_near(0, 1)
-    backward(1)
-    for f in range(2):
-        inputs(1, f)
-        inputs(0, f)
     reduce_far(1, 0)
     reduce_far(1, 1)
     weight_grads(0)
+    second_hop(1)
+    backward(1)
+    inputs(1, 0)
+    inputs(1, 1)
     reduce_near(1, 0)
     reduce_near(1, 1)
     combine(0, 0)
@@ -595,9 +601,22 @@
         pltpu.make_async_copy(grads.at[n], out, out_sem.at[n]).wait()
 
 
-def deliver(mixed_in, igrad_in, rgrad_in, gg_in, gu_in, gd_in, *outs):
-    for src, dst in zip((mixed_in, igrad_in, rgrad_in, gg_in, gu_in, gd_in), outs):
-        dst[...] = src[...]
+def deliver(
+    mixed_in, igrad_in, rgrad_in, gg_in, gu_in, gd_in,
+    mixed_out, igrad_out, rgrad_out, gg_out, gu_out, gd_out, sem,
+):
+    pairs = ((gg_in, gg_out), (gu_in, gu_out), (gd_in, gd_out))
+    writes = []
+    for n, (src, dst) in enumerate(pairs):
+        for e in range(4):
+            writes.append(pltpu.make_async_copy(src.at[e], dst.at[e], sem.at[n, e]))
+    for write in writes:
+        write.start()
+    mixed_out[...] = mixed_in[...]
+    igrad_out[...] = igrad_in[...]
+    rgrad_out[...] = rgrad_in[...]
+    for write in writes:
+        write.wait()
 
 
 def on_device(tokens, output_grad, router_logits, expert_ids, w_gate, w_up, w_down):
@@ -605,10 +624,12 @@
     vmem = pl.BlockSpec(memory_space=pltpu.VMEM)
     dma = pltpu.SemaphoreType.DMA
     weight = jax.ShapeDtypeStruct((4, D, HID), BF16)
+    kept = pltpu.VMEM((4, D, HID), BF16)
+    part_kept = pltpu.VMEM((BLK, TOK), BF16)
     block = jax.ShapeDtypeStruct((BLK, TOK), BF16)
     mixed, igrad, rgrad, gg, gu, gd = pl.pallas_call(
         kernel,
-        out_shape=(block, block, jax.ShapeDtypeStruct((4, TOK), F32), weight, weight, weight),
+        out_shape=(part_kept, part_kept, pltpu.VMEM((4, TOK), F32), kept, kept, kept),
         in_specs=[anywhere, anywhere, vmem, vmem, anywhere, anywhere, anywhere],
         out_specs=(vmem, vmem, vmem, anywhere, anywhere, anywhere),
         scratch_shapes=[
@@ -656,7 +677,7 @@
             dma((3,)),
         ],
         compiler_params=pltpu.CompilerParams(
-            collective_id=0, has_side_effects=True, vmem_limit_bytes=58 * 2**20
+            collective_id=0, has_side_effects=True, vmem_limit_bytes=59 * 2**20
         ),
         cost_estimate=pl.CostEstimate(
             flops=2 * 9 * 640 * D * HID, bytes_accessed=9 * 10**6, transcendentals=640 * HID
@@ -666,15 +687,13 @@
         tokens.T, output_grad.T, router_logits.T, expert_ids.T,
         w_gate, w_up, jnp.swapaxes(w_down, 1, 2),
     )
-    small = pl.BlockSpec((BLK, TOK), lambda e: (0, 0))
-    tiny = pl.BlockSpec((4, TOK), lambda e: (0, 0))
-    large = pl.BlockSpec((1, D, HID), lambda e: (e, 0, 0))
     mixed, igrad, rgrad, gg, gu, gd = pl.pallas_call(
         deliver,
-        grid=(4,),
         out_shape=(block, block, jax.ShapeDtypeStruct((4, TOK), F32), weight, weight, weight),
-        in_specs=[small, small, tiny, large, large, large],
-        out_specs=(small, small, tiny, large, large, large),
+        in_specs=[vmem, vmem, vmem, vmem, vmem, vmem],
+        out_specs=(vmem, vmem, vmem, anywhere, anywhere, anywhere),
+        scratch_shapes=[dma((3, 4))],
+        compiler_params=pltpu.CompilerParams(vmem_limit_bytes=16 * 2**20),
         cost_estimate=pl.CostEstimate(flops=0, bytes_accessed=9 * 10**6, transcendentals=0),
         name="deliver",
     )(mixed, igrad, rgrad, gg, gu, gd)

time: 73.3 us -> 64.5 us (0.88)
  Pallas kernels: 72.5 us -> 63.7 us
    pallas_call x2, Pallas kernels: 72.5 us -> 63.7 us  [the longest x1 60.9 us: on_device(): pl.pallas_call(kernel, out_shape=(part_kept, part_kept, pltpu.VMEM((4, TO...]
where the time goes in v3:
time: 64.5 us; the launch traced here: 64.4 us
  Pallas kernels  63.7 us (99%)
    pallas_call x1, Pallas kernels, on_device(): pl.pallas_call(kernel, out_shape=(part_kept, part_kept, pltpu.VMEM((4, TO...  60.9 us
    pallas_call x1, Pallas kernels, on_device(): pl.pallas_call(deliver, out_shape=(block, block, jax.ShapeDtypeStruct((4,...  2.8 us

profile of v3, /device:TPU:1, one launch (start us, length us, event | category | flops | bytes accessed | tf_op | source)
XLA Modules:
  0.0 64.4 jit_solution(11379963223776653084)
XLA Ops:
  0.6 60.9 %moe_layer.1 = (bf16[90,128]{1,0:T(8,128)(2,1)S(1)}, bf16[90,128]{1,0:T(8,128)(2,1)S(1)}, f32[4,128]{1,0:T(4,128)S(1)}, bf16[4,1440,128]{2,1,0:T(8,128)(2,1)S(1)...) custom-call(bf16[1440,128]{1,0:T(8,128)(2,1)} %bitcast.11, bf16[1440,128]{1,0:T(8,128)(2,1)} %bitcast.12, ...), custom_call_target="tpu_custom_call" | custom-call | flops 2123366400 | bytes 9000000 | tf_op jit(solution)/shard_map/moe_layer/pallas_call | solution.py:630
  61.6 2.8 %deliver.1 = (bf16[90,128]{1,0:T(8,128)(2,1)}, bf16[90,128]{1,0:T(8,128)(2,1)}, f32[4,128]{1,0:T(4,128)}, bf16[4,1440,128]{2,1,0:T(8,128)(2,1)}, bf16[4,1440,128...) custom-call(bf16[90,128]{1,0:T(8,128)(2,1)S(1)} %get-tuple-element.18.mixed_in, ...), custom_call_target="tpu_custom_call" | custom-call | bytes 9000000 | tf_op jit(solution)/shard_map/deliver/pallas_call | solution.py:690

commit v4 on v3

--- a/solution.py
+++ b/solution.py
@@ -221,17 +221,19 @@
     for e in range(4):
         wgu[e, pl.ds(D, WIDE - HALF), :] = jnp.zeros((WIDE - HALF, 2 * HID), BF16)
         wd[e, pl.ds(D, WIDE - HALF), :] = jnp.zeros((WIDE - HALF, HID), BF16)
-    main, main_w = select(main_back, spot - RANKS * second)
-    fold, fold_w = select(fold_back, 6 + (spot & 3))
-    comb_hi[0] = main_w.astype(BF16)
-    comb_lo[0] = (main_w - main_w.astype(BF16).astype(F32)).astype(BF16)
+    for o in range(2):
+        if o == 1:
+            main, main_w = select(main_back, spot - RANKS * second)
+            fold, fold_w = select(fold_back, 6 + (spot & 3))
+        comb_hi[o, 0] = main_w.astype(BF16)
+        comb_lo[o, 0] = (main_w - main_w.astype(BF16).astype(F32)).astype(BF16)
+        for k in range(3):
+            w_here = jnp.where((spot >> 2) == k, fold_w, 0.0)
+            comb_hi[o, 1 + k] = w_here.astype(BF16)
+            comb_lo[o, 1 + k] = (w_here - w_here.astype(BF16).astype(F32)).astype(BF16)
     comb_one[0] = ones_where(main)
     for k in range(3):
-        here = (spot >> 2) == k
-        w_here = jnp.where(here, fold_w, 0.0)
-        comb_hi[1 + k] = w_here.astype(BF16)
-        comb_lo[1 + k] = (w_here - w_here.astype(BF16).astype(F32)).astype(BF16)
-        comb_one[1 + k] = ones_where(fold & here)
+        comb_one[1 + k] = ones_where(fold & ((spot >> 2) == k))
 
     n = iota((PAIR, 256), 0)
     i = iota((PAIR, 256), 1)
@@ -361,57 +363,64 @@
         loop(0, 2, body)
         to_core(1, f, o).start()
 
-    def across(a, f, le):
-        return pltpu.make_async_remote_copy(
-            src_ref=zsend.at[a, f, le], dst_ref=zrecv.at[a, f, le],
-            send_sem=rz_s.at[a], recv_sem=rz_r.at[a, f],
+    def across(f, le):
+        return pltpu.make_async_remote_copy(
+            src_ref=zsend.at[f, le], dst_ref=zrecv.at[f, le],
+            send_sem=rz_s, recv_sem=rz_r.at[f],
             device_id=up if le == 0 else down, device_id_type=MESH,
         )
 
-    def reduce_far(a, f):
-        to_core(a, f, 0).wait_recv()
+    def reduce_far(f):
+        to_core(1, f, 0).wait_recv()
         for le in range(2):
             r = pl.ds(le * ROWS, ROWS)
-            total = part[a, 0, f, 0, r, :].astype(F32) + crecv[a, f, 0, r, :].astype(F32)
-            zsend[a, f, le] = total.astype(BF16)
-            across(a, f, le).start()
-
-    def give_back(a, f, i):
-        return pltpu.make_async_remote_copy(
-            src_ref=slab.at[a, f, slab_rows(peer(i))],
-            dst_ref=back.at[a, f, slab_rows(me)],
-            send_sem=bk_s.at[a, f], recv_sem=bk_r.at[a, f],
+            total = part[1, 0, f, 0, r, :].astype(F32) + crecv[1, f, 0, r, :].astype(F32)
+            zsend[f, le] = total.astype(BF16)
+            across(f, le).start()
+
+    def give_back(ch, f, i):
+        return pltpu.make_async_remote_copy(
+            src_ref=slab.at[ch, f, slab_rows(peer(i))],
+            dst_ref=back.at[ch, f, slab_rows(me)],
+            send_sem=bk_s.at[ch, f], recv_sem=bk_r.at[ch, f],
             device_id=(d, peer(i)), device_id_type=MESH,
         )
 
-    def all_back(a, f):
+    def all_back(ch, f):
         fifteen = pl.ds(0, 15 * SLAB)
         return pltpu.make_async_remote_copy(
-            src_ref=slab.at[a, f, fifteen], dst_ref=back.at[a, f, fifteen],
-            send_sem=bk_s.at[a, f], recv_sem=bk_r.at[a, f],
-            device_id=sib, device_id_type=MESH,
-        )
-
-    def reduce_near(a, f):
-        to_core(a, f, 1).wait_recv()
+            src_ref=slab.at[ch, f, fifteen], dst_ref=back.at[ch, f, fifteen],
+            send_sem=bk_s.at[ch, f], recv_sem=bk_r.at[ch, f],
+            device_id=sib, device_id_type=MESH,
+        )
+
+    def across_all(f):
+        return pltpu.make_async_remote_copy(
+            src_ref=zsend.at[f], dst_ref=zrecv.at[f],
+            send_sem=rz_s, recv_sem=rz_r.at[f],
+            device_id=up, device_id_type=MESH,
+        )
+
+    def reduce_near(ch, f):
+        a, o = ((0, 0), (0, 1), (1, 1))[ch]
+        to_core(a, f, o).wait_recv()
+        if ch == 2:
+            across_all(f).wait_recv()
         totals = []
-        pltpu.make_async_remote_copy(
-            src_ref=zsend.at[a, f], dst_ref=zrecv.at[a, f],
-            send_sem=rz_s.at[a], recv_sem=rz_r.at[a, f],
-            device_id=up, device_id_type=MESH,
-        ).wait_recv()
         for le in range(2):
             r = pl.ds(le * ROWS, ROWS)
-            total = part[a, 0, f, 1, r, :].astype(F32) + crecv[a, f, 1, r, :].astype(F32)
-            totals.append((total + zrecv[a, f, le].astype(F32)).astype(BF16))
+            total = part[a, 0, f, o, r, :].astype(F32) + crecv[a, f, o, r, :].astype(F32)
+            if ch == 2:
+                total += zrecv[f, le].astype(F32)
+            totals.append(total.astype(BF16))
         both = jnp.concatenate(totals, 0)
-        slab[a, f, :, 0:PART] = dg(ungrp[0], both, 1, 0).astype(BF16)
+        slab[ch, f, :, 0:PART] = dg(ungrp[0], both, 1, 0).astype(BF16)
         folded = jnp.zeros((256, TOK), F32)
         for k in range(3):
             folded += dg(ungrp[1 + k], both[:, k * TOK : (k + 1) * TOK], 1, 0)
-        slab[a, f, :, PART:BACK] = folded.astype(BF16)
-        back[a, f, slab_rows(me), :] = slab[a, f, slab_rows(me), :]
-        loop(1, 16, lambda i: give_back(a, f, i).start())
+        slab[ch, f, :, PART:BACK] = folded.astype(BF16)
+        back[ch, f, slab_rows(me), :] = slab[ch, f, slab_rows(me), :]
+        loop(1, 16, lambda i: give_back(ch, f, i).start())
 
     def block_owner(k):
         return (4 * c + k // 2) * 2 + k % 2
@@ -445,11 +454,12 @@
         )
 
     def combine(a, f):
-        all_back(a, f).wait_recv()
+        for ch in (0, 1) if a == 0 else (2,):
+            all_back(ch, f).wait_recv()
         if a == 1 and f == 1:
-            main_dot = back[1, 1, :, DOT_LANE : DOT_LANE + 1].astype(F32)
+            main_dot = back[2, 1, :, DOT_LANE : DOT_LANE + 1].astype(F32)
             lane = DOT_LANE + TOK
-            fold_dot = back[1, 1, :, lane : lane + 1].astype(F32)
+            fold_dot = back[2, 1, :, lane : lane + 1].astype(F32)
             main_dot = jnp.where(comb_one[0].astype(F32) > 0.5, main_dot, 0.0)
             fold_dot = jnp.where(comb_one[3].astype(F32) > 0.5, fold_dot, 0.0)
             lines = []
@@ -459,12 +469,15 @@
                 lines.append(jnp.sum(mine_p, 0, keepdims=True))
             dots[d] = jnp.concatenate(lines + [jnp.zeros((4, TOK), F32)], 0)
             loop(1, 16, lambda i: tell(i).start())
-        tables = (comb_hi, comb_lo) if a == 0 else (comb_one,)
+        if a == 0:
+            tables = [(t.at[o], o) for o in range(2) for t in (comb_hi, comb_lo)]
+        else:
+            tables = [(comb_one, 2)]
         value = jnp.zeros((TOK, PART), F32)
-        for table in tables:
-            value += dg(table[0], back[a, f, :, 0:PART], 0, 0)
+        for table, ch in tables:
+            value += dg(table[0], back[ch, f, :, 0:PART], 0, 0)
             value += jnp.concatenate(
-                [dg(table[1 + k], back[a, f, :, PART:BACK], 0, 0) for k in range(3)], 1
+                [dg(table[1 + k], back[ch, f, :, PART:BACK], 0, 0) for k in range(3)], 1
             )
         total = dg(blksel[f], value.astype(BF16), 1, 1).astype(BF16)
         for k in range(4):
@@ -527,29 +540,29 @@
     outputs(0, 1)
     second_hop(0)
     first_hop(1, 0, 5)
-    reduce_far(0, 0)
-    reduce_far(0, 1)
     forward(1)
     first_hop(1, 5, 10)
     outputs(1, 0)
     outputs(1, 1)
+    reduce_near(0, 0)
     first_hop(1, 10, 15)
     backward(0)
     inputs(0, 0)
     inputs(0, 1)
-    reduce_near(0, 0)
     reduce_near(0, 1)
-    reduce_far(1, 0)
-    reduce_far(1, 1)
-    weight_grads(0)
+    reduce_far(0)
+    reduce_far(1)
+    reduce_near(1, 0)
+    reduce_near(1, 1)
     second_hop(1)
     backward(1)
     inputs(1, 0)
     inputs(1, 1)
-    reduce_near(1, 0)
-    reduce_near(1, 1)
+    reduce_near(2, 0)
+    reduce_near(2, 1)
     combine(0, 0)
     combine(0, 1)
+    weight_grads(0)
     weight_grads(1)
     combine(1, 0)
     combine(1, 1)
@@ -563,6 +576,10 @@
     rgrad_ref[...] = dot - weights * jnp.sum(dot, 0, keepdims=True)
 
     told().wait_send()
+    for f in range(2):
+        across_all(f).wait_send()
+        for ch in range(3):
+            all_back(ch, f).wait_send()
     for a in range(2):
         fifteen = pl.ds(0, 15 * SLAB)
         pltpu.make_async_remote_copy(
@@ -580,14 +597,8 @@
             send_sem=rc_s.at[a], recv_sem=rc_r.at[a, 0, 0],
             device_id=sib, device_id_type=MESH,
         ).wait_send()
-        pltpu.make_async_remote_copy(
-            src_ref=zsend.at[a], dst_ref=zrecv.at[a],
-            send_sem=rz_s.at[a], recv_sem=rz_r.at[a, 0],
-            device_id=sib, device_id_type=MESH,
-        ).wait_send()
         for f in range(2):
             from_sibling(a, f).wait_send()
-            all_back(a, f).wait_send()
 
         @pl.when(inside)
         def _():
@@ -642,8 +653,8 @@
             pltpu.VMEM((2, 2, PAIR, PADDED), BF16),
             pltpu.VMEM((256, TOK), BF16),
             pltpu.VMEM((256, 3 * TOK), BF16),
-            pltpu.VMEM((4, 256, TOK), BF16),
-            pltpu.VMEM((4, 256, TOK), BF16),
+            pltpu.VMEM((2, 4, 256, TOK), BF16),
+            pltpu.VMEM((2, 4, 256, TOK), BF16),
             pltpu.VMEM((4, 256, TOK), BF16),
             pltpu.VMEM((4, PAIR, 256), BF16),
             pltpu.VMEM((4, 256, PAIR), BF16),
@@ -657,10 +668,10 @@
             pltpu.VMEM((2, PAIR, HID), F32),
             pltpu.VMEM((2, 2, 2, 2, PAIR, PART), BF16),
             pltpu.VMEM((2, 2, 2, PAIR, PART), BF16),
-            pltpu.VMEM((2, 2, 2, ROWS, PART), BF16),
-            pltpu.VMEM((2, 2, 2, ROWS, PART), BF16),
-            pltpu.VMEM((2, 2, 256, BACK), BF16),
-            pltpu.VMEM((2, 2, 256, BACK), BF16),
+            pltpu.VMEM((2, 2, ROWS, PART), BF16),
+            pltpu.VMEM((2, 2, ROWS, PART), BF16),
+            pltpu.VMEM((3, 2, 256, BACK), BF16),
+            pltpu.VMEM((3, 2, 256, BACK), BF16),
             pltpu.VMEM((2, 8, BROWS, TOK), BF16),
             pltpu.VMEM((2, 8, BROWS, TOK), BF16),
             pltpu.VMEM((16, 8, TOK), F32),
@@ -670,8 +681,8 @@
             dma((2,)), dma((2, 2)),
             dma((2, 2)), dma((2, 2)),
             dma((2,)), dma((2, 2, 2)),
-            dma((2,)), dma((2, 2)),
-            dma((2, 2)), dma((2, 2)),
+            dma(()), dma((2,)),
+            dma((3, 2)), dma((3, 2)),
             dma((2,)), dma((2,)),
             dma(()), dma(()),
             dma((3,)),

time: 64.5 us -> 64.9 us (level)
  no operation moved by 1% of the time
where the time goes in v4:
time: 64.9 us; the launch traced here: 64.7 us
  Pallas kernels  64.1 us (99%)
    pallas_call x1, Pallas kernels, on_device(): pl.pallas_call(kernel, out_shape=(part_kept, part_kept, pltpu.VMEM((4, TO...  61.3 us
    pallas_call x1, Pallas kernels, on_device(): pl.pallas_call(deliver, out_shape=(block, block, jax.ShapeDtypeStruct((4,...  2.8 us

profile of v4, /device:TPU:1, one launch (start us, length us, event | category | flops | bytes accessed | tf_op | source)
XLA Modules:
  0.0 64.7 jit_solution(15533117089929716184)
XLA Ops:
  0.6 61.3 %moe_layer.1 = (bf16[90,128]{1,0:T(8,128)(2,1)S(1)}, bf16[90,128]{1,0:T(8,128)(2,1)S(1)}, f32[4,128]{1,0:T(4,128)S(1)}, bf16[4,1440,128]{2,1,0:T(8,128)(2,1)S(1)...) custom-call(bf16[1440,128]{1,0:T(8,128)(2,1)} %bitcast.11, bf16[1440,128]{1,0:T(8,128)(2,1)} %bitcast.12, ...), custom_call_target="tpu_custom_call" | custom-call | flops 2123366400 | bytes 9000000 | tf_op jit(solution)/shard_map/moe_layer/pallas_call | solution.py:641
  61.9 2.8 %deliver.1 = (bf16[90,128]{1,0:T(8,128)(2,1)}, bf16[90,128]{1,0:T(8,128)(2,1)}, f32[4,128]{1,0:T(4,128)}, bf16[4,1440,128]{2,1,0:T(8,128)(2,1)}, bf16[4,1440,128...) custom-call(bf16[90,128]{1,0:T(8,128)(2,1)S(1)} %get-tuple-element.18.mixed_in, ...), custom_call_target="tpu_custom_call" | custom-call | bytes 9000000 | tf_op jit(solution)/shard_map/deliver/pallas_call | solution.py:701

commit v5 on v3

--- a/solution.py
+++ b/solution.py
@@ -411,7 +411,7 @@
             folded += dg(ungrp[1 + k], both[:, k * TOK : (k + 1) * TOK], 1, 0)
         slab[a, f, :, PART:BACK] = folded.astype(BF16)
         back[a, f, slab_rows(me), :] = slab[a, f, slab_rows(me), :]
-        loop(1, 16, lambda i: give_back(a, f, i).start())
+        loop(0, 15, lambda j: give_back(a, f, turn(14 - j)).start())
 
     def block_owner(k):
         return (4 * c + k // 2) * 2 + k % 2

time: 64.5 us -> 64 us (level)
  no operation moved by 1% of the time
where the time goes in v5:
time: 64 us; the launch traced here: 63.9 us
  Pallas kernels  63.3 us (99%)
  between operations  0.64 us (1%)
    pallas_call x1, Pallas kernels, on_device(): pl.pallas_call(kernel, out_shape=(part_kept, part_kept, pltpu.VMEM((4, TO...  60.5 us
    pallas_call x1, Pallas kernels, on_device(): pl.pallas_call(deliver, out_shape=(block, block, jax.ShapeDtypeStruct((4,...  2.8 us

profile of v5, /device:TPU:1, one launch (start us, length us, event | category | flops | bytes accessed | tf_op | source)
XLA Modules:
  0.0 63.9 jit_solution(5515919483796228230)
XLA Ops:
  0.6 60.5 %moe_layer.1 = (bf16[90,128]{1,0:T(8,128)(2,1)S(1)}, bf16[90,128]{1,0:T(8,128)(2,1)S(1)}, f32[4,128]{1,0:T(4,128)S(1)}, bf16[4,1440,128]{2,1,0:T(8,128)(2,1)S(1)...) custom-call(bf16[1440,128]{1,0:T(8,128)(2,1)} %bitcast.11, bf16[1440,128]{1,0:T(8,128)(2,1)} %bitcast.12, ...), custom_call_target="tpu_custom_call" | custom-call | flops 2123366400 | bytes 9000000 | tf_op jit(solution)/shard_map/moe_layer/pallas_call | solution.py:630
  61.1 2.8 %deliver.1 = (bf16[90,128]{1,0:T(8,128)(2,1)}, bf16[90,128]{1,0:T(8,128)(2,1)}, f32[4,128]{1,0:T(4,128)}, bf16[4,1440,128]{2,1,0:T(8,128)(2,1)}, bf16[4,1440,128...) custom-call(bf16[90,128]{1,0:T(8,128)(2,1)S(1)} %get-tuple-element.18.mixed_in, ...), custom_call_target="tpu_custom_call" | custom-call | bytes 9000000 | tf_op jit(solution)/shard_map/deliver/pallas_call | solution.py:690
